TPU v7x, 128 devices: a whole 4x4x4 slice. The times are simulated.
128 devices in a mesh: row: 8 (over z_lo, x), col: 16 (over z_hi, y, core).
Axes of the slice: x: 4, y: 4, z: 4 (z_hi: 2, z_lo: 2; z = z_hi * 2 + z_lo), core: 2. Of those that a mesh axis runs over, the one named last changes fastest.
Arguments:
- single: bfloat16 [1536, 384], P('row'), may hold values from -6 to 6
- res_bin: int32 [1536, 1536], P('row', 'col'), may hold values from 0 to 65
- tok_bin: int32 [1536, 1536], P('row', 'col'), may hold values from 0 to 65
- chain_ids: int32 [1536], replicated, may hold values from 0 to 7, as said below
- w_rows: bfloat16 [384, 128], replicated, may hold values from -0.3125 to 0.3125
- w_cols: bfloat16 [384, 128], replicated, may hold values from -0.3125 to 0.3125
- rel_table: bfloat16 [138, 128], replicated, may hold values from -3 to 3
- ln_gain: float32 [128], replicated, may hold values from 0.5 to 1.5
- ln_bias: float32 [128], replicated, may hold values from -3 to 3
- w_in: bfloat16 [128, 512], replicated, may hold values from -0.5 to 0.5
- cot_ab: bfloat16 [1536, 1536, 256], P('row', 'col'), may hold values from -0.1875 to 0.1875
- cot_z: bfloat16 [1536, 1536, 128], P('row', 'col'), may hold values from -0.1875 to 0.1875
Outputs:
- grad_single: float32 [1536, 384], P('row')
- grad_w_rows: float32 [384, 128], replicated
- grad_w_cols: float32 [384, 128], replicated
- grad_table: float32 [138, 128], replicated
- grad_gain: float32 [128], replicated
- grad_bias: float32 [128], replicated
- grad_w_in: float32 [128, 512], replicated
Inputs may be any that keep to these rules, and one draw needn't show every extreme that they name: `chain_ids`: token-to-chain ids of the crop: never falling along the tokens, the first token in chain 0 and the last in chain 8 - 1.
All inputs are finite; a program needn't handle non-finite values.
Results may differ from a plain program's by a relative error of at most 0.0062.
Values may be sent and summed in bfloat16 or wider, within the bound.
No kernel may reach another device: no remote copies, remote signals or barrier semaphores. Data moves between devices by JAX's collectives and lax.ppermute only.
A program may use at most 128 MiB of HBM per device.

v0:
```python
import jax
import jax.numpy as jnp
from jax import lax
from jax.sharding import PartitionSpec as P

RBINS = 66
NBINS = 138


def broadcast(value, axis, source):
    kept = jnp.where(lax.axis_index(axis) == source, value, 0).astype(value.dtype)
    return lax.psum(kept, axis)


def pair_features(res_rows, tok_rows, chain_left, chain_right):
    offset_bin = jnp.clip(chain_left[:, None] - chain_right[None, :] + 2, 0, 4) + 2 * RBINS
    same_bin = jnp.where(chain_left[:, None] == chain_right[None, :], 2 * RBINS + 5, -1)
    bin_ids = jnp.arange(NBINS, dtype=jnp.int32)
    multi_hot = (bin_ids == res_rows[..., None]) | (bin_ids == tok_rows[..., None] + RBINS)
    multi_hot = multi_hot | (bin_ids == offset_bin[..., None]) | (bin_ids == same_bin[..., None])
    return multi_hot.astype(jnp.float32)


def contract_rows(left, right):
    return lax.dot_general(
        left,
        right,
        (((0,), (0,)), ((), ())),
        precision=lax.Precision.HIGHEST,
        preferred_element_type=jnp.float32,
    )


def block_backward(
    row_proj,
    col_proj,
    res_rows,
    tok_rows,
    chain_left,
    chain_right,
    cot_edges,
    cot_pair,
    rel_table,
    ln_gain,
    ln_bias,
    w_in,
):
    height = row_proj.shape[0]
    width = col_proj.shape[0]
    channels = row_proj.shape[1]
    hidden = w_in.shape[1] // 4
    flat_hot = pair_features(res_rows, tok_rows, chain_left, chain_right).reshape(
        height * width, -1
    )
    relative = jnp.dot(flat_hot.astype(jnp.bfloat16), rel_table, preferred_element_type=jnp.float32)
    relative = relative.reshape(height, width, channels)
    pair = (row_proj[:, None, :] + col_proj[None, :, :] + relative).astype(jnp.bfloat16)
    pair_wide = pair.astype(jnp.float32).reshape(height * width, channels)
    centre = jnp.mean(pair_wide, axis=-1, keepdims=True)
    centred = pair_wide - centre
    variance = jnp.mean(centred * centred, axis=-1, keepdims=True)
    inv_std = lax.rsqrt(variance + 1e-05)
    standard = centred * inv_std
    normed = (standard * ln_gain + ln_bias).astype(jnp.bfloat16)
    projected = jnp.dot(normed, w_in, preferred_element_type=jnp.float32)
    gate_a = projected[:, :hidden]
    value_a = projected[:, hidden : 2 * hidden]
    gate_b = projected[:, 2 * hidden : 3 * hidden]
    value_b = projected[:, 3 * hidden :]
    cot_wide = cot_edges.reshape(height * width, 2 * hidden).astype(jnp.float32)
    cot_a = cot_wide[:, :hidden]
    cot_b = cot_wide[:, hidden:]
    sig_a = jax.nn.sigmoid(gate_a)
    sig_b = jax.nn.sigmoid(gate_b)
    proj_grad = jnp.concatenate(
        [
            cot_a * value_a * sig_a * (1.0 - sig_a),
            cot_a * sig_a,
            cot_b * value_b * sig_b * (1.0 - sig_b),
            cot_b * sig_b,
        ],
        axis=-1,
    ).astype(jnp.bfloat16)
    normed_grad = lax.dot_general(
        proj_grad, w_in, (((1,), (1,)), ((), ())), preferred_element_type=jnp.float32
    )
    grad_w_in = lax.dot_general(
        normed, proj_grad, (((0,), (0,)), ((), ())), preferred_element_type=jnp.float32
    )
    grad_gain = jnp.sum(normed_grad * standard, axis=0)
    grad_bias = jnp.sum(normed_grad, axis=0)
    scaled = normed_grad * ln_gain
    pair_grad = cot_pair.reshape(height * width, channels).astype(jnp.float32) + inv_std * (
        scaled
        - jnp.mean(scaled, axis=-1, keepdims=True)
        - standard * jnp.mean(scaled * standard, axis=-1, keepdims=True)
    )
    grad_table = contract_rows(flat_hot, pair_grad)
    grid_grad = pair_grad.reshape(height, width, channels)
    return (
        grad_w_in,
        grad_gain,
        grad_bias,
        grad_table,
        jnp.sum(grid_grad, axis=1),
        jnp.sum(grid_grad, axis=0),
    )


def per_device(
    single,
    res_bin,
    tok_bin,
    chain_ids,
    w_rows,
    w_cols,
    rel_table,
    ln_gain,
    ln_bias,
    w_in,
    cot_ab,
    cot_z,
):
    row_tok, col_tok = res_bin.shape
    channels = w_rows.shape[1]
    col_ratio = lax.axis_size("col") // lax.axis_size("row")
    row_at = lax.axis_index("row")
    col_at = lax.axis_index("col")
    owner_row = col_at // col_ratio
    offset = col_at % col_ratio * col_tok
    proj_rows = jnp.dot(single, w_rows, preferred_element_type=jnp.float32)
    local_cols = jnp.dot(
        lax.dynamic_slice_in_dim(single, offset, col_tok, 0),
        w_cols,
        preferred_element_type=jnp.float32,
    )
    proj_cols = broadcast(local_cols, "row", owner_row)
    chain_left = lax.dynamic_slice_in_dim(chain_ids, row_at * row_tok, row_tok, 0)
    chain_right = lax.dynamic_slice_in_dim(chain_ids, col_at * col_tok, col_tok, 0)
    candidates = [
        member
        for member in range(1, row_tok + 1)
        if row_tok % member == 0 and member * col_tok >= 4096
    ]
    row_step = candidates[0] if candidates else row_tok
    block_count = row_tok // row_step
    inputs = (
        proj_rows.reshape(block_count, row_step, channels),
        res_bin.reshape(block_count, row_step, col_tok),
        tok_bin.reshape(block_count, row_step, col_tok),
        chain_left.reshape(block_count, row_step),
        cot_ab.reshape(block_count, row_step, col_tok, cot_ab.shape[2]),
        cot_z.reshape(block_count, row_step, col_tok, channels),
    )

    def visit(carry, pieces):
        results = block_backward(
            pieces[0],
            proj_cols,
            pieces[1],
            pieces[2],
            pieces[3],
            chain_right,
            pieces[4],
            pieces[5],
            rel_table,
            ln_gain,
            ln_bias,
            w_in,
        )
        carry = (
            carry[0] + results[0],
            carry[1] + results[1],
            carry[2] + results[2],
            carry[3] + results[3],
            carry[4] + results[5],
        )
        return (carry, results[4])

    zeros_init = (
        jnp.zeros(w_in.shape, jnp.float32),
        jnp.zeros((channels,), jnp.float32),
        jnp.zeros((channels,), jnp.float32),
        jnp.zeros(rel_table.shape, jnp.float32),
        jnp.zeros((col_tok, channels), jnp.float32),
    )
    carry, row_parts = lax.scan(visit, zeros_init, inputs)
    partial_rows = row_parts.reshape(row_tok, channels)
    partial_cols = carry[4]
    row_grad = lax.psum(partial_rows, "col")
    col_block = lax.psum(partial_cols, "row")
    every = lax.all_gather(col_block, "col", axis=0, tiled=True)
    col_grad = lax.dynamic_slice_in_dim(every, row_at * row_tok, row_tok, 0)
    singles_wide = single.astype(jnp.float32)
    grad_w_rows, grad_w_cols = lax.psum(
        (contract_rows(singles_wide, row_grad), contract_rows(singles_wide, col_grad)), "row"
    )
    grad_w_in, grad_gain, grad_bias, grad_table = lax.psum(
        (carry[0], carry[1], carry[2], carry[3]), ("row", "col")
    )
    grad_single = lax.dot_general(
        row_grad,
        w_rows.astype(jnp.float32),
        (((1,), (1,)), ((), ())),
        precision=lax.Precision.HIGHEST,
        preferred_element_type=jnp.float32,
    )
    grad_single = grad_single + lax.dot_general(
        col_grad,
        w_cols.astype(jnp.float32),
        (((1,), (1,)), ((), ())),
        precision=lax.Precision.HIGHEST,
        preferred_element_type=jnp.float32,
    )
    return (grad_single, grad_w_rows, grad_w_cols, grad_table, grad_gain, grad_bias, grad_w_in)


def solution(mesh):
    in_specs = (
        P("row", None),
        P("row", "col"),
        P("row", "col"),
        P(),
        P(),
        P(),
        P(),
        P(),
        P(),
        P(),
        P("row", "col", None),
        P("row", "col", None),
    )
    out_specs = (P("row", None), P(), P(), P(), P(), P(), P())
    return jax.shard_map(
        per_device, mesh=mesh, in_specs=in_specs, out_specs=out_specs, check_vma=False
    )
```

profile of v0, /device:TPU:1, one launch (start us, length us, event | category | flops | bytes accessed | tf_op | source)
XLA Modules:
  0.0 613.5 jit_solution(4175850676267838782)
XLA Ops:
  9.1 28.8 %psum.63 = f32[96,128]{1,0:T(8,128)S(1)} all-reduce(f32[96,128]{1,0:T(8,128)S(1)} %convolution_select_fusion), channel_id=1, replica_groups=mesh['row'=8,'col'=16] {'row'}, use_global_device_ids=true, to_apply=%region_0.1 | all-reduce | flops 12288 | bytes 98304 | tf_op jit(solution)/shard_map/psum | solution.py:12
  40.7 198.1 %while.21 = (s32[]{:T(128)}, f32[128,512]{1,0:T(8,128)S(1)}, f32[128]{0:T(128)S(1)}, f32[128]{0:T(128)S(1)}, f32[138,128]{1,0:T(8,128)S(1)}, /*index=5*/f32[96,1...) while((s32[]{:T(128)}, f32[128,512]{1,0:T(8,128)S(1)}, ...), condition=%wide.region_10.11_spmd.clone, body=%wide.region_1.10_spmd.clone.sunk | while | flops 3034439424 | bytes 143248432 | solution.py:187
  41.6 3.3 convert_reduce_fusion.2
  44.9 1.6 multiply_reduce_fusion.6
  46.8 2.5 add_convert_fusion.3
  49.3 5.0 fusion.87
  54.3 1.8 constant_dynamic-slice_fusion.6
  56.7 2.5 fusion.86
  59.2 3.1 copy.33
  62.3 3.0 copy.34
  65.3 6.0 fusion.88
  71.4 4.3 multiply_reduce_fusion.7
  77.1 5.2 convert_add_fusion.2
  82.7 4.1 fusion.91
  88.5 1.7 convolution_add_fusion.3
  91.1 3.3 convert_reduce_fusion.2
  94.4 1.6 multiply_reduce_fusion.6
  96.2 2.5 add_convert_fusion.3
  98.8 5.0 fusion.87
  103.8 1.8 constant_dynamic-slice_fusion.6
  106.2 2.5 fusion.86
  108.7 3.1 copy.33
  111.8 3.0 copy.34
  114.8 6.0 fusion.88
  120.9 4.3 multiply_reduce_fusion.7
  126.6 5.2 convert_add_fusion.2
  132.2 4.1 fusion.91
  137.9 1.7 convolution_add_fusion.3
  140.6 3.3 convert_reduce_fusion.2
  143.9 1.6 multiply_reduce_fusion.6
  145.7 2.5 add_convert_fusion.3
  148.2 5.0 fusion.87
  153.3 1.8 constant_dynamic-slice_fusion.6
  155.6 2.5 fusion.86
  158.2 3.1 copy.33
  161.2 3.0 copy.34
  164.3 6.0 fusion.88
  170.4 4.3 multiply_reduce_fusion.7
  176.1 5.2 convert_add_fusion.2
  181.7 4.1 fusion.91
  187.4 1.7 convolution_add_fusion.3
  190.0 3.3 convert_reduce_fusion.2
  193.4 1.6 multiply_reduce_fusion.6
  195.2 2.5 add_convert_fusion.3
  197.7 5.0 fusion.87
  202.8 1.8 constant_dynamic-slice_fusion.6
  205.1 2.5 fusion.86
  207.6 3.1 copy.33
  210.7 3.0 copy.34
  213.8 6.0 fusion.88
  219.8 4.3 multiply_reduce_fusion.7
  225.6 5.2 convert_add_fusion.2
  231.2 4.1 fusion.91
  236.9 1.7 convolution_add_fusion.3
  238.9 24.2 %psum.65 = f32[96,128]{1,0:T(8,128)S(1)} all-reduce(f32[96,128]{1,0:T(8,128)S(1)} %get-tuple-element.110), channel_id=1, replica_groups=mesh['row'=8,'col'=16] {'row'}, use_global_device_ids=true, to_apply=%region_12.13 | all-reduce | flops 12288 | bytes 98304 | tf_op jit(solution)/shard_map/psum | solution.py:191
  263.1 41.7 %all_gather.3 = f32[1536,128]{1,0:T(8,128)S(1)} all-gather(f32[96,128]{1,0:T(8,128)S(1)} %psum.65), channel_id=1, replica_groups=mesh['row'=8,'col'=16] {'col'}, dimensions={0}, use_global_device_ids=true | all-gather | bytes 835584 | tf_op jit(solution)/shard_map/all_gather | solution.py:192
  305.8 70.1 %all-reduce.7.cloned.1.call-done = f32[192,128]{1,0:T(8,128)} async-done(((f32[192,128]{1,0:T(8,128)}), f32[192,128]{1,0:T(8,128)}) %all-reduce.7.cloned.1.call-update) | async-done | bytes 98320 | tf_op jit(solution)/shard_map/psum | solution.py:190
  375.9 1.9 convolution_bitcast_fusion.1
  378.6 68.1 %all-reduce = (f32[128]{0:T(128)}, f32[128]{0:T(128)}) all-reduce(f32[128]{0:T(128)S(1)} %get-tuple-element.112, f32[128]{0:T(128)S(1)} %get-tuple-element.113), channel_id=1, replica_groups=mesh['row'=8,'col'=16] {'row','col'}, use_global_device_ids=true, to_apply=%region_16.17 | all-reduce | flops 256 | bytes 2048 | tf_op jit(solution)/shard_map/psum | solution.py:198
  450.1 1.7 copy.27
  451.8 1.7 copy.28
  453.6 150.3 %all-reduce.9.cloned.1.call-done = (f32[138,128]{1,0:T(8,128)}, f32[128,512]{1,0:T(8,128)}) async-done(((f32[138,128]{1,0:T(8,128)}, f32[128,512]{1,0:T(8,128)}), (f32[138,128]{1,0:T(8,128)}, f32[128,512]{1,0:T(8,128)})) %all-reduce.9.cloned.1.call-update) | async-done | bytes 332816 | tf_op jit(solution)/shard_map/psum | solution.py:198
  603.8 1.5 copy.62
  605.3 1.7 copy.63
  (223 shorter events, 29.5 us)
Async XLA Ops:
  7.2 0.9 copy-start
  7.2 368.7 %all-reduce.7.cloned.1.call-start = ((), (), s32[]{:S(2)}) async-start(), calls=%async_computation | async-start | bytes 196608 | tf_op jit(solution)/shard_map/psum | solution.py:190
  41.6 5.2 copy-start.15
  41.6 5.2 copy-start.16
  44.9 4.4 copy-start.10
  71.3 4.4 copy-start.2
  71.4 4.4 copy-start.4
  71.4 4.4 copy-start.6
  71.4 4.4 copy-start.8
  82.7 4.1 copy-start.1
  82.7 5.2 copy-start.7
  82.7 5.2 copy-start.9
  86.8 1.3 copy-start.3
  86.8 1.6 copy-start.5
  91.0 5.2 copy-start.15
  91.1 5.2 copy-start.16
  94.4 4.4 copy-start.10
  120.8 4.4 copy-start.2
  120.8 4.4 copy-start.4
  120.8 4.4 copy-start.6
  120.9 4.4 copy-start.8
  132.2 4.1 copy-start.1
  132.2 5.2 copy-start.7
  132.2 5.2 copy-start.9
  136.3 1.3 copy-start.3
  136.3 1.6 copy-start.5
  140.5 5.2 copy-start.15
  140.5 5.2 copy-start.16
  143.9 4.4 copy-start.10
  170.3 4.4 copy-start.2
  170.3 4.4 copy-start.4
  170.3 4.4 copy-start.6
  170.3 4.4 copy-start.8
  181.7 4.1 copy-start.1
  181.7 5.2 copy-start.7
  181.7 5.2 copy-start.9
  185.8 1.3 copy-start.3
  185.8 1.6 copy-start.5
  190.0 5.2 copy-start.15
  190.0 5.2 copy-start.16
  193.3 4.4 copy-start.10
  219.8 4.4 copy-start.2
  219.8 4.4 copy-start.4
  219.8 4.4 copy-start.6
  219.8 4.4 copy-start.8
  231.2 4.1 copy-start.1
  231.2 5.2 copy-start.7
  231.2 5.2 copy-start.9
  235.3 1.3 copy-start.3
  235.3 1.6 copy-start.5
  238.8 139.1 %copy-start.13 = (f32[128,512]{1,0:T(8,128)}, f32[128,512]{1,0:T(8,128)S(1)}, u32[]{:S(2)}) copy-start(f32[128,512]{1,0:T(8,128)S(1)} %get-tuple-element.114) | copy-start | bytes 786436
  238.8 139.1 %copy-start.14 = (f32[138,128]{1,0:T(8,128)}, f32[138,128]{1,0:T(8,128)S(1)}, u32[]{:S(2)}) copy-start(f32[138,128]{1,0:T(8,128)S(1)} %get-tuple-element.111) | copy-start | bytes 211972
  238.8 207.9 %copy-start.12 = (bf16[384,128]{1,0:T(8,128)(2,1)S(1)}, bf16[384,128]{1,0:T(8,128)(2,1)}, u32[]{:S(2)}) copy-start(bf16[384,128]{1,0:T(8,128)(2,1)} %param.18) | copy-start | bytes 294916
  238.8 209.1 %copy-start.11 = (bf16[384,128]{1,0:T(8,128)(2,1)S(1)}, bf16[384,128]{1,0:T(8,128)(2,1)}, u32[]{:S(2)}) copy-start(bf16[384,128]{1,0:T(8,128)(2,1)} %param.19) | copy-start | bytes 294916
  238.9 211.2 %all-reduce.11.cloned.1.call-start = ((), (), s32[]{:S(2)}) async-start(), calls=%async_computation.2 | async-start | bytes 786432 | tf_op jit(solution)/shard_map/psum | solution.py:195
  377.8 226.0 %all-reduce.9.cloned.1.call-start = ((), (), s32[]{:S(2)}) async-start(), calls=%async_computation.1 | async-start | bytes 671744 | tf_op jit(solution)/shard_map/psum | solution.py:198
Sparse Core Ops, SparseCore 0:
  239.0 136.8 all-reduce.6
  379.2 70.8 all-reduce.10
  455.6 148.1 all-reduce.8
where the time goes:
time: 615 us; the launch traced here: 614 us
  waiting for transfers between devices  222 us (36%)
  blocking collectives  163 us (27%)
  matrix products  81 us (13%)
  other arithmetic  68.7 us (11%)
  local copies, waits for them, and re-layouts  63.4 us (10%)
  between operations  14 us (2%)
    psum x1, waiting for transfers between devices, per_device(): lax.psum((carry[0], carry[1], carry[2], carry[3]), ('row', 'col'))  150 us
    psum x1, waiting for transfers between devices, per_device(): row_grad = lax.psum(partial_rows, 'col')  70.1 us
    psum x1, blocking collectives, per_device(): lax.psum((carry[0], carry[1], carry[2], carry[3]), ('row', 'col'))  68.1 us
    all_gather x1, blocking collectives, per_device(): every = lax.all_gather(col_block, 'col', axis=0, tiled=True)  41.7 us
    psum x1, blocking collectives, broadcast(): return lax.psum(kept, axis)  28.8 us
    while x104, local copies, waits for them, and re-layouts  26.8 us
    psum x1, blocking collectives, per_device(): col_block = lax.psum(partial_cols, 'row')  24.2 us
    another operation x4, other arithmetic  24.1 us
  transfers between devices with their start and end apart: 3, of which 3 were waited for; matrix products, arithmetic and copies ran while one was open for 1% of the time, Pallas kernels for 0%

commit v1 on v0

v1 whole, which is shorter than its diff:
```python
import jax
import jax.numpy as jnp
from jax import lax
from jax.experimental import pallas as pl
from jax.experimental.pallas import tpu as pltpu
from jax.sharding import PartitionSpec as P

RBINS = 66
SLOT = 72
HOT = 2 * SLOT
NCHAIN = 8
BOTH = ("row", "col")
ROWS = 8
GROUP = 4

BF = jnp.bfloat16
F32 = jnp.float32


def dot(left, right, dims=((1,), (0,))):
    return lax.dot_general(left, right, (dims, ((), ())), preferred_element_type=F32)


def split_dot(left, right):
    high = right.astype(BF)
    low = (right - high.astype(F32)).astype(BF)
    return dot(left, high, ((0,), (0,))) + dot(left, low, ((0,), (0,)))


def pair_kernel(
    chain_left,
    bins,
    cot_ab,
    cot_z,
    single_rows,
    single_cols,
    chain_right,
    w_rows,
    w_cols,
    table,
    table_chain,
    gain_ref,
    bias_ref,
    w_in,
    sums,
    row_sums,
    col_sums,
    w_fwd,
    w_back,
    averager,
    proj_rows,
    base,
    col_acc,
    gw_acc,
    table_acc,
    gain_acc,
    bias_acc,
):
    step = pl.program_id(0)
    width = cot_z.shape[1]
    channels = cot_z.shape[2]
    hidden = channels
    gain = gain_ref[...]
    bias = bias_ref[...]

    @pl.when(step == 0)
    def _():
        wide = w_in[...].astype(F32)
        lane = lax.broadcasted_iota(jnp.int32, wide.shape, 1)
        is_gate = (lane // hidden) % 2 == 0
        w_fwd[...] = jnp.where(is_gate, wide * 0.5, wide).astype(BF)
        back = jnp.transpose(wide * jnp.where(is_gate, 0.25, 0.5))
        w_back[:, :channels] = back.astype(BF)
        mean = jnp.mean(back * gain, axis=1, keepdims=True)
        w_back[:, channels:] = jnp.broadcast_to(mean, back.shape).astype(BF)
        averager[...] = jnp.full((channels, channels), 1.0 / channels, BF)
        proj_rows[...] = dot(single_rows[...], w_rows[...])
        cols = dot(single_cols[...], w_cols[...])
        for chain in range(NCHAIN):
            offset = jnp.clip(chain - chain_right[...] + 2, 0, 4)
            value = cols
            for place in range(5):
                value = value + jnp.where(offset == place, table_chain[place : place + 1, :], 0.0)
            same = chain_right[...] == chain
            base[chain] = value + jnp.where(same, table_chain[5:6, :], 0.0)
        col_acc[...] = jnp.zeros_like(col_acc)
        gw_acc[...] = jnp.zeros_like(gw_acc)
        table_acc[...] = jnp.zeros_like(table_acc)
        gain_acc[...] = jnp.zeros_like(gain_acc)
        bias_acc[...] = jnp.zeros_like(bias_acc)

    pairs = GROUP * width
    bin_ids = lax.broadcasted_iota(jnp.int32, (SLOT, pairs), 0)
    proj_block = proj_rows[pl.ds(pl.multiple_of(step * ROWS, ROWS), ROWS), :]
    ones = averager[...]
    row_list = []
    for at in range(0, ROWS, GROUP):
        span = slice(at * width, at * width + pairs)
        res_hot = jnp.where(bin_ids == bins[0, 0:1, span], 1.0, 0.0)
        tok_hot = jnp.where(bin_ids == bins[0, 1:2, span], 1.0, 0.0)
        hot = jnp.concatenate([res_hot, tok_hot], axis=0).astype(BF)
        relative = dot(hot, table[...], ((0,), (0,))).reshape(GROUP, width, channels)
        chains = [chain_left[step * ROWS + at + k] for k in range(GROUP)]
        pair = jnp.concatenate(
            [
                relative[k] + base[chains[k]] + proj_block[at + k : at + k + 1, :]
                for k in range(GROUP)
            ],
            axis=0,
        ).astype(BF)
        centred = pair.astype(F32) - dot(pair, ones)
        variance = dot((centred * centred).astype(BF), ones)
        inv_std = lax.rsqrt(variance + 1e-05)
        standard = centred * inv_std
        normed = (standard * gain + bias).astype(BF)
        projected = dot(normed, w_fwd[...])
        parts = []
        for edge in range(2):
            begin = 2 * hidden * edge
            tanh = jnp.tanh(projected[:, begin : begin + hidden])
            value = projected[:, begin + hidden : begin + 2 * hidden]
            cot = cot_ab[at : at + GROUP, :, edge * hidden : (edge + 1) * hidden]
            cot = cot.reshape(pairs, hidden).astype(F32)
            double = cot + cot * tanh
            quad = double * value
            parts.append((quad - quad * tanh).astype(BF))
            parts.append(double.astype(BF))
        proj_grad = jnp.concatenate(parts, axis=1)
        gw_acc[...] += dot(normed, proj_grad, ((0,), (0,)))
        back = dot(proj_grad, w_back[...])
        normed_grad = back[:, :channels]
        product = normed_grad * standard
        gain_acc[...] += jnp.sum(product.reshape(pairs // 8, 8, channels), axis=0)
        bias_acc[...] += jnp.sum(normed_grad.reshape(pairs // 8, 8, channels), axis=0)
        scaled = normed_grad * gain - back[:, channels:]
        slope = dot((scaled * standard).astype(BF), ones)
        residual = cot_z[at : at + GROUP].reshape(pairs, channels).astype(F32)
        pair_grad = residual + inv_std * (scaled - standard * slope)
        table_acc[...] += dot(hot, pair_grad.astype(BF))
        grid = pair_grad.reshape(GROUP, width, channels)
        for k in range(GROUP):
            col_acc[chains[k]] += grid[k]
            row_list.append(jnp.sum(grid[k], axis=0, keepdims=True))
    row_sums[pl.ds(pl.multiple_of(step * ROWS, ROWS), ROWS), :] = jnp.concatenate(row_list, axis=0)

    @pl.when(step == pl.num_programs(0) - 1)
    def _():
        for part in range(4):
            scale = 0.25 if part % 2 == 0 else 0.5
            block = gw_acc[:, part * hidden : (part + 1) * hidden]
            sums[part * channels : (part + 1) * channels, :] = block * scale
        at = 4 * channels
        sums[at : at + HOT, :] = table_acc[...]
        total = jnp.zeros((width, channels), F32)
        places = [jnp.zeros((1, channels), F32) for _ in range(6)]
        for chain in range(NCHAIN):
            value = col_acc[chain]
            total = total + value
            offset = jnp.clip(chain - chain_right[...] + 2, 0, 4)
            for place in range(5):
                kept = jnp.where(offset == place, value, 0.0)
                places[place] = places[place] + jnp.sum(kept, axis=0, keepdims=True)
            kept = jnp.where(chain_right[...] == chain, value, 0.0)
            places[5] = places[5] + jnp.sum(kept, axis=0, keepdims=True)
        col_sums[...] = total
        for place in range(6):
            sums[at + RBINS + place : at + RBINS + place + 1, :] = places[place]
        spare = at + SLOT + RBINS
        sums[spare : spare + 1, :] = jnp.sum(gain_acc[...], axis=0, keepdims=True)
        sums[spare + 1 : spare + 2, :] = jnp.sum(bias_acc[...], axis=0, keepdims=True)
        at = at + HOT
        depth = single_rows.shape[1]
        sums[at : at + depth, :] = split_dot(single_rows[...], row_sums[...])
        at = at + depth
        sums[at : at + depth, :] = split_dot(single_cols[...], total)
        at = at + depth
        sums[at:, :] = jnp.zeros((sums.shape[0] - at, channels), F32)


def pair_work(chain_left, bins, cot_ab, cot_z, single, single_cols, chain_right, w_rows, w_cols, table, table_chain, gain, bias, w_in, padded):
    row_tok, col_tok, channels = cot_z.shape
    whole = pl.BlockSpec(memory_space=pltpu.VMEM)
    steps = row_tok // ROWS
    return pl.pallas_call(
        pair_kernel,
        grid=(steps,),
        in_specs=[
            pl.BlockSpec(memory_space=pltpu.SMEM),
            pl.BlockSpec((1, 2, ROWS * col_tok), lambda i: (i, 0, 0)),
            pl.BlockSpec((ROWS, col_tok, 2 * channels), lambda i: (i, 0, 0)),
            pl.BlockSpec((ROWS, col_tok, channels), lambda i: (i, 0, 0)),
        ]
        + [whole] * 10,
        out_specs=[whole, whole, whole],
        out_shape=[
            jax.ShapeDtypeStruct((padded, channels), F32),
            jax.ShapeDtypeStruct((row_tok, channels), F32),
            jax.ShapeDtypeStruct((col_tok, channels), F32),
        ],
        scratch_shapes=[
            pltpu.VMEM((channels, 4 * channels), BF),
            pltpu.VMEM((4 * channels, 2 * channels), BF),
            pltpu.VMEM((channels, channels), BF),
            pltpu.VMEM((row_tok, channels), F32),
            pltpu.VMEM((NCHAIN, col_tok, channels), F32),
            pltpu.VMEM((NCHAIN, col_tok, channels), F32),
            pltpu.VMEM((channels, 4 * channels), F32),
            pltpu.VMEM((HOT, channels), F32),
            pltpu.VMEM((8, channels), F32),
            pltpu.VMEM((8, channels), F32),
        ],
        compiler_params=pltpu.CompilerParams(vmem_limit_bytes=50 * 1024 * 1024),
        cost_estimate=pl.CostEstimate(
            flops=9 * 10**9, bytes_accessed=15 * 10**6, transcendentals=7 * 10**6
        ),
    )(chain_left, bins, cot_ab, cot_z, single, single_cols, chain_right, w_rows, w_cols, table, table_chain, gain, bias, w_in)


def turned(row, col):
    z_lo, x = row // 4, row % 4
    z_hi, y, core = col // 8, col // 2 % 4, col % 2
    return z_hi * 4 + y, z_lo * 8 + (x + 2) % 4 * 2 + core


def turn_pairs():
    pairs = []
    for row in range(8):
        for col in range(16):
            to_row, to_col = turned(row, col)
            pairs.append((row * 16 + col, to_row * 16 + to_col))
    return pairs


def swap(value, mask):
    return lax.ppermute(value, BOTH, [(at, at ^ mask) for at in range(128)])


def pick(value, place):
    half = value.shape[0] // 2
    return lax.dynamic_slice_in_dim(value, place * half, half, 0)


def halve(value, place, mask):
    got = swap(pick(value, 1 - place).astype(BF), mask)
    return pick(value, place) + got.astype(F32)


def both_sum(value, mask):
    return value + swap(value, mask)


def double(value, place, mask):
    got = swap(value, mask)
    first = jnp.where(place == 0, value, got)
    second = jnp.where(place == 0, got, value)
    return jnp.concatenate([first, second], axis=0)


def per_device(
    single,
    res_bin,
    tok_bin,
    chain_ids,
    w_rows,
    w_cols,
    rel_table,
    ln_gain,
    ln_bias,
    w_in,
    cot_ab,
    cot_z,
):
    row_tok, col_tok = res_bin.shape
    channels = w_rows.shape[1]
    depth = single.shape[1]
    row_at = lax.axis_index("row")
    col_at = lax.axis_index("col")
    core = col_at % 2
    y_at = col_at // 2 % 4
    y_half = (y_at % 2) ^ (y_at // 2)
    x_at = row_at % 4
    x_half = (x_at % 2) ^ (x_at // 2)
    turn = turn_pairs()

    single_cols = lax.ppermute(pick(single, core), BOTH, [(to, at) for at, to in turn])
    chain_left = lax.dynamic_slice_in_dim(chain_ids, row_at * row_tok, row_tok, 0)
    chain_right = lax.dynamic_slice_in_dim(chain_ids, col_at * col_tok, col_tok, 0)
    chain_right = jnp.broadcast_to(chain_right[:, None], (col_tok, channels))
    steps = row_tok // ROWS
    bins = jnp.stack(
        [res_bin.reshape(steps, ROWS * col_tok), tok_bin.reshape(steps, ROWS * col_tok)], axis=1
    )
    gap = jnp.zeros((SLOT - RBINS, channels), rel_table.dtype)
    table = jnp.concatenate([rel_table[:RBINS], gap, rel_table[RBINS : 2 * RBINS], gap], axis=0)
    table_chain = jnp.pad(rel_table[2 * RBINS :].astype(F32), ((0, 2), (0, 0)))
    used = 4 * channels + HOT + 2 * depth
    padded = -(-used // 128) * 128
    sums, row_sums, col_sums = pair_work(
        chain_left,
        bins,
        cot_ab,
        cot_z,
        single,
        single_cols,
        chain_right,
        w_rows,
        w_cols,
        table,
        table_chain,
        ln_gain[None, :],
        ln_bias[None, :],
        w_in,
        padded,
    )
    cols = lax.ppermute(col_sums.astype(BF), BOTH, turn).astype(F32)
    halves = jnp.concatenate([sums.reshape(2, padded // 2, channels), row_sums.reshape(2, row_tok // 2, channels)], axis=1)
    held = halve(halves.reshape(padded + row_tok, channels), core, 1)
    weights, rows = held[: padded // 2], held[padded // 2 :]
    quarter = padded // 4
    tok = row_tok // 4
    mixed = jnp.concatenate(
        [
            weights.reshape(2, quarter, channels),
            rows.reshape(2, tok, channels),
            cols.reshape(2, tok, channels),
        ],
        axis=1,
    )
    held = halve(mixed.reshape(-1, channels), y_half, 2)
    weights, tokens = halve(held[:quarter], x_half, 16), held[quarter:]
    eighth = quarter // 2
    held = jnp.concatenate([weights, tokens], axis=0)
    held = both_sum(held, 6)
    held = both_sum(held, 8)
    weights, tokens = held[:eighth], held[eighth:]
    weights = both_sum(weights, 48)
    weights = both_sum(weights, 64)
    weights = double(weights.astype(BF), x_half, 16)
    done = jnp.concatenate([weights, tokens.astype(BF)], axis=0)
    done = double(done, y_half, 2)
    done = double(done, core, 1)
    done = done.reshape(2, 2, quarter + 2 * tok, channels)
    weights = done[:, :, :quarter].reshape(padded, channels)
    rows = done[:, :, quarter : quarter + tok].reshape(row_tok, channels)
    cols = done[:, :, quarter + tok :].reshape(row_tok, channels)
    grad_single = dot(
        jnp.concatenate([rows, cols], axis=1),
        jnp.concatenate([w_rows, w_cols], axis=1),
        ((1,), (1,)),
    )
    weights = weights.astype(F32)
    at = 4 * channels
    grad_w_in = weights[:at].reshape(4, channels, channels).transpose(1, 0, 2)
    grad_w_in = grad_w_in.reshape(channels, at)
    spare = at + SLOT + RBINS
    grad_table = jnp.concatenate(
        [
            weights[at : at + RBINS],
            weights[at + SLOT : spare],
            weights[at + RBINS : at + SLOT],
        ],
        axis=0,
    )
    grad_gain = weights[spare]
    grad_bias = weights[spare + 1]
    at = at + HOT
    grad_w_rows = weights[at : at + depth]
    grad_w_cols = weights[at + depth : at + 2 * depth]
    return (grad_single, grad_w_rows, grad_w_cols, grad_table, grad_gain, grad_bias, grad_w_in)


def solution(mesh):
    in_specs = (
        P("row", None),
        P("row", "col"),
        P("row", "col"),
        P(),
        P(),
        P(),
        P(),
        P(),
        P(),
        P(),
        P("row", "col", None),
        P("row", "col", None),
    )
    out_specs = (P("row", None), P(), P(), P(), P(), P(), P())
    return jax.shard_map(
        per_device, mesh=mesh, in_specs=in_specs, out_specs=out_specs, check_vma=False
    )
```

time: 615 us -> 137 us (0.22)
  waiting for transfers between devices: 222 us -> 27.1 us
  blocking collectives: 163 us -> 0 us
  matrix products: 81 us -> 0.95 us
  other arithmetic: 68.7 us -> 1.36 us
  Pallas kernels: 0 us -> 63.7 us
  local copies, waits for them, and re-layouts: 63.4 us -> 13.4 us
  starting transfers between devices: 0.12 us -> 28.6 us
  between operations: 14 us -> 0.95 us
    psum x3 -> x0, waiting for transfers between devices: 222 us -> none  [the longest x1 150 us: per_device(): lax.psum((carry[0], carry[1], carry[2], carry[3]), ('row', 'col'))]
    psum x3 -> x0, blocking collectives: 121 us -> none  [the longest x1 68.1 us: per_device(): lax.psum((carry[0], carry[1], carry[2], carry[3]), ('row', 'col'))]
    dot_general x26 -> x1, matrix products: 81 us -> 0.95 us  [dot(): lax.dot_general(left, right, (dims, ((), ())), preferred_element_type=F32)]
    pallas_call x0 -> x1, Pallas kernels: none -> 63.7 us  [pair_work(): pl.pallas_call(pair_kernel, grid=(steps,), in_specs=[pl.BlockSpec(memory_...]
    all_gather x1 -> x0, blocking collectives: 41.7 us -> none  [per_device(): every = lax.all_gather(col_block, 'col', axis=0, tiled=True)]
    ppermute x0 -> x12, starting transfers between devices: none -> 28.6 us  [the longest x10 24.6 us: swap(): return lax.ppermute(value, BOTH, [(at, at ^ mask) for at in range(128)])]
    ppermute x0 -> x12, waiting for transfers between devices: none -> 27.1 us  [the longest x10 23.3 us: swap(): return lax.ppermute(value, BOTH, [(at, at ^ mask) for at in range(128)])]
    while x104 -> x0, local copies, waits for them, and re-layouts: 26.8 us -> none
  transfers between devices with their start and end apart: 3 -> 12, of which waited for: 3 -> 10; matrix products, arithmetic and copies ran while one was open for 1% -> 4% of each run, Pallas kernels for 0% -> 0%
where the time goes in v1:
time: 137 us; the launch traced here: 136 us
  Pallas kernels  63.7 us (46%)
  starting transfers between devices  28.6 us (21%)
  waiting for transfers between devices  27.1 us (20%)
  local copies, waits for them, and re-layouts  13.4 us (10%)
    pallas_call x1, Pallas kernels, pair_work(): pl.pallas_call(pair_kernel, grid=(steps,), in_specs=[pl.BlockSpec(memory_...  63.7 us
    ppermute x10, starting transfers between devices, swap(): return lax.ppermute(value, BOTH, [(at, at ^ mask) for at in range(128)])  24.6 us
    ppermute x10, waiting for transfers between devices, swap(): return lax.ppermute(value, BOTH, [(at, at ^ mask) for at in range(128)])  23.3 us
    unnamed x17, local copies, waits for them, and re-layouts  5.65 us
    ppermute x1, waiting for transfers between devices, per_device(): cols = lax.ppermute(col_sums.astype(BF), BOTH, turn).astype(F32)  3.77 us
    ppermute x1, starting transfers between devices, per_device(): lax.ppermute(pick(single, core), BOTH, [(to, at) for at, to in turn])  3.57 us
  transfers between devices with their start and end apart: 12, of which 10 were waited for; matrix products, arithmetic and copies ran while one was open for 4% of the time, Pallas kernels for 0%

profile of v1, /device:TPU:1, one launch (start us, length us, event | category | flops | bytes accessed | tf_op | source)
XLA Modules:
  0.0 136.1 jit_solution(7845939133158502726)
XLA Ops:
  0.7 0.9 constant_dynamic-slice_fusion
  1.5 3.6 %collective-permute-start = (bf16[96,384]{1,0:T(8,128)(2,1)S(1)}, bf16[96,384]{1,0:T(8,128)(2,1)S(1)}, u32[]{:S(2)}, u32[]{:S(2)}) collective-permute-start(bf16[96,384]{1,0:T(8,128)(2,1)S(1)} %constant_dynamic-slice_fusion), channel_id=1, source_target_pairs={{4,0},{5,1},{20,2},{21,3},{36,4},{37,5},{52,6},{53,7},{68,8},{69,9... | collective-permute-start | bytes 221192 | tf_op jit(solution)/shard_map/ppermute | solution.py:285
  5.1 0.8 fusion.12
  5.9 0.7 slice.63
  6.6 1.0 stack_reshape.7
  7.7 1.0 stack_reshape.6
  8.7 0.8 dynamic_slice.27.chain_left
  9.5 0.8 dynamic_slice.29
  10.3 0.1 pad_add_fusion.bins
  10.4 0.0 collective-permute-done.single_cols
  10.5 0.1 broadcast_in_dim.15.chain_right
  10.5 0.0 copy-start
  10.5 0.9 copy-done
  11.4 0.0 copy-start.2
  11.4 0.9 copy-done.2
  12.3 0.0 copy-start.4
  12.3 0.9 copy-done.4
  13.2 0.0 copy-start.5
  13.2 0.9 copy-done.5
  14.1 0.0 copy-start.6
  14.1 0.7 copy-done.6
  14.8 0.0 copy-start.7
  14.8 0.7 copy-done.7
  15.4 63.7 %shard_map.171 = (f32[1536,128]{1,0:T(8,128)S(1)}, f32[192,128]{1,0:T(8,128)S(1)}, f32[96,128]{1,0:T(8,128)S(1)}) custom-call(s32[192]{0:T(256)S(1)} %dynamic_slice.27.chain_left, s32[24,2,768]{2,1,0:T(2,128)S(1)} %pad_add_fusion.bins, bf16[192,96,256]{2,1,0:T(8,128)(2,1)} %cot_ab.1, bf16[192,96,128]{2,1,0:T(8,128)(2,1)} %cot_z.1, ...), custom_call_target="tpu_custom_call" | custom-call | flops 8999999488 | bytes 15000000 | tf_op jit(solution)/shard_map/pallas_call | solution.py:184
  79.1 0.0 copy-start.1
  79.2 0.0 copy-start.3
  79.2 0.1 pad_maximum_fusion
  79.3 1.0 collective-permute-start.1
  80.3 0.4 collective-permute-start.2
  80.7 3.8 %collective-permute-done.2 = bf16[96,128]{1,0:T(8,128)(2,1)S(1)} collective-permute-done((bf16[96,128]{1,0:T(8,128)(2,1)S(1)}, bf16[96,128]{1,0:T(8,128)(2,1)S(1)}, u32[]{:S(2)}, u32[]{:S(2)}) %collective-permute-start.2) | collective-permute-done | bytes 24608 | tf_op jit(solution)/shard_map/ppermute | solution.py:315
  84.5 0.0 collective-permute-done.1
  84.5 0.1 convert_add_fusion
  84.7 1.6 %collective-permute-start.3 = (bf16[480,128]{1,0:T(8,128)(2,1)S(1)}, bf16[480,128]{1,0:T(8,128)(2,1)S(1)}, u32[]{:S(2)}, u32[]{:S(2)}) collective-permute-start(bf16[480,128]{1,0:T(8,128)(2,1)S(1)} %dynamic-slice_convert_fusion.1), channel_id=1, source_target_pairs={{0,2},{1,3},{2,0},{3,1},{4,6},{5,7},{6,4},{7,5},{8,10},{9,11},{10,... | collective-permute-start | bytes 368648 | tf_op jit(solution)/shard_map/ppermute | solution.py:235
  86.3 2.3 %collective-permute-done.3 = bf16[480,128]{1,0:T(8,128)(2,1)S(1)} collective-permute-done((bf16[480,128]{1,0:T(8,128)(2,1)S(1)}, bf16[480,128]{1,0:T(8,128)(2,1)S(1)}, u32[]{:S(2)}, u32[]{:S(2)}) %collective-permute-start.3) | collective-permute-done | bytes 122912 | tf_op jit(solution)/shard_map/ppermute | solution.py:235
  88.7 0.1 collective-permute-start.4
  88.8 2.9 %collective-permute-done.4 = bf16[192,128]{1,0:T(8,128)(2,1)S(1)} collective-permute-done((bf16[192,128]{1,0:T(8,128)(2,1)S(1)}, bf16[192,128]{1,0:T(8,128)(2,1)S(1)}, u32[]{:S(2)}, u32[]{:S(2)}) %collective-permute-start.4) | collective-permute-done | bytes 49184 | tf_op jit(solution)/shard_map/ppermute | solution.py:235
  91.7 2.3 %collective-permute-start.5 = (f32[288,128]{1,0:T(8,128)S(1)}, f32[288,128]{1,0:T(8,128)S(1)}, u32[]{:S(2)}, u32[]{:S(2)}) collective-permute-start(f32[288,128]{1,0:T(8,128)S(1)} %pad_maximum_fusion.4), channel_id=1, source_target_pairs={{0,6},{1,7},{2,4},{3,5},{4,2},{5,3},{6,0},{7,1},{8,14},{9,15},{10,... | collective-permute-start | bytes 442376 | tf_op jit(solution)/shard_map/ppermute | solution.py:235
  94.0 3.0 %collective-permute-done.5 = f32[288,128]{1,0:T(8,128)S(1)} collective-permute-done((f32[288,128]{1,0:T(8,128)S(1)}, f32[288,128]{1,0:T(8,128)S(1)}, u32[]{:S(2)}, u32[]{:S(2)}) %collective-permute-start.5) | collective-permute-done | bytes 147488 | tf_op jit(solution)/shard_map/ppermute | solution.py:235
  97.0 5.8 %collective-permute-start.6 = (f32[288,128]{1,0:T(8,128)S(1)}, f32[288,128]{1,0:T(8,128)S(1)}, u32[]{:S(2)}, u32[]{:S(2)}) collective-permute-start(f32[288,128]{1,0:T(8,128)S(1)} %fusion.8), channel_id=1, source_target_pairs={{0,8},{1,9},{2,10},{3,11},{4,12},{5,13},{6,14},{7,15},{8,0},{9,1},... | collective-permute-start | bytes 442376 | tf_op jit(solution)/shard_map/ppermute | solution.py:235
  102.8 2.5 %collective-permute-done.6 = f32[288,128]{1,0:T(8,128)S(1)} collective-permute-done((f32[288,128]{1,0:T(8,128)S(1)}, f32[288,128]{1,0:T(8,128)S(1)}, u32[]{:S(2)}, u32[]{:S(2)}) %collective-permute-start.6) | collective-permute-done | bytes 147488 | tf_op jit(solution)/shard_map/ppermute | solution.py:235
  105.4 2.1 %collective-permute-start.7 = (f32[192,128]{1,0:T(8,128)S(1)}, f32[192,128]{1,0:T(8,128)S(1)}, u32[]{:S(2)}, u32[]{:S(2)}) collective-permute-start(f32[192,128]{1,0:T(8,128)S(1)} %slice.85), channel_id=1, source_target_pairs={{0,48},{1,49},{2,50},{3,51},{4,52},{5,53},{6,54},{7,55},{8,56},{9,... | collective-permute-start | bytes 294920 | tf_op jit(solution)/shard_map/ppermute | solution.py:235
  107.5 2.6 %collective-permute-done.7 = f32[192,128]{1,0:T(8,128)S(1)} collective-permute-done((f32[192,128]{1,0:T(8,128)S(1)}, f32[192,128]{1,0:T(8,128)S(1)}, u32[]{:S(2)}, u32[]{:S(2)}) %collective-permute-start.7) | collective-permute-done | bytes 98336 | tf_op jit(solution)/shard_map/ppermute | solution.py:235
  110.2 1.8 %collective-permute-start.8 = (f32[192,128]{1,0:T(8,128)S(1)}, f32[192,128]{1,0:T(8,128)S(1)}, u32[]{:S(2)}, u32[]{:S(2)}) collective-permute-start(f32[192,128]{1,0:T(8,128)S(1)} %slice_add_fusion), channel_id=1, source_target_pairs={{0,64},{1,65},{2,66},{3,67},{4,68},{5,69},{6,70},{7,71},{8,72},{9,... | collective-permute-start | bytes 294920 | tf_op jit(solution)/shard_map/ppermute | solution.py:235
  112.0 2.0 %collective-permute-done.8 = f32[192,128]{1,0:T(8,128)S(1)} collective-permute-done((f32[192,128]{1,0:T(8,128)S(1)}, f32[192,128]{1,0:T(8,128)S(1)}, u32[]{:S(2)}, u32[]{:S(2)}) %collective-permute-start.8) | collective-permute-done | bytes 98336 | tf_op jit(solution)/shard_map/ppermute | solution.py:235
  114.0 0.1 collective-permute-start.9
  114.1 2.9 %collective-permute-done.9 = bf16[192,128]{1,0:T(8,128)(2,1)S(1)} collective-permute-done((bf16[192,128]{1,0:T(8,128)(2,1)S(1)}, bf16[192,128]{1,0:T(8,128)(2,1)S(1)}, u32[]{:S(2)}, u32[]{:S(2)}) %collective-permute-start.9) | collective-permute-done | bytes 49184 | tf_op jit(solution)/shard_map/ppermute | solution.py:235
  117.1 0.1 collective-permute-start.10
  117.2 4.0 %collective-permute-done.10 = bf16[480,128]{1,0:T(8,128)(2,1)S(1)} collective-permute-done((bf16[480,128]{1,0:T(8,128)(2,1)S(1)}, bf16[480,128]{1,0:T(8,128)(2,1)S(1)}, u32[]{:S(2)}, u32[]{:S(2)}) %collective-permute-start.10) | collective-permute-done | bytes 122912 | tf_op jit(solution)/shard_map/ppermute | solution.py:235
  121.1 0.1 broadcast_select_fusion.3
  121.2 9.7 %collective-permute-start.11 = (bf16[960,128]{1,0:T(8,128)(2,1)S(1)}, bf16[960,128]{1,0:T(8,128)(2,1)S(1)}, u32[]{:S(2)}, u32[]{:S(2)}) collective-permute-start(bf16[960,128]{1,0:T(8,128)(2,1)S(1)} %pad_maximum_fusion.3), channel_id=1, source_target_pairs={{0,1},{1,0},{2,3},{3,2},{4,5},{5,4},{6,7},{7,6},{8,9},{9,8},{10,11... | collective-permute-start | bytes 737288 | tf_op jit(solution)/shard_map/ppermute | solution.py:235
  130.9 1.1 collective-permute-done.11
  132.0 0.1 broadcast_select_fusion.1
  132.2 0.1 bitcast_convert_fusion
  132.3 0.8 fusion.10
  133.1 0.5 slice_bitcast_fusion
  133.6 0.2 copy.19
  133.8 0.7 copy.22
  134.5 0.0 copy-done.1
  134.5 0.0 copy-done.3
  134.5 1.0 fusion
  135.5 0.6 pad_maximum_fusion.6
  (31 shorter events, 0.4 us)
Async XLA Ops:
  1.5 8.9 %collective-permute-start = (bf16[96,384]{1,0:T(8,128)(2,1)S(1)}, bf16[96,384]{1,0:T(8,128)(2,1)S(1)}, u32[]{:S(2)}, u32[]{:S(2)}) collective-permute-start(bf16[96,384]{1,0:T(8,128)(2,1)S(1)} %constant_dynamic-slice_fusion), channel_id=1, source_target_pairs={{4,0},{5,1},{20,2},{21,3},{36,4},{37,5},{52,6},{53,7},{68,8},{69,9... | collective-permute-start | bytes 221192 | tf_op jit(solution)/shard_map/ppermute | solution.py:285
  10.5 0.9 copy-start
  11.4 0.9 copy-start.2
  12.3 0.9 copy-start.4
  13.2 0.9 copy-start.5
  14.1 0.7 copy-start.6
  14.8 0.7 copy-start.7
  79.1 55.4 %copy-start.1 = (bf16[384,128]{1,0:T(8,128)(2,1)S(1)}, bf16[384,128]{1,0:T(8,128)(2,1)}, u32[]{:S(2)}) copy-start(bf16[384,128]{1,0:T(8,128)(2,1)} %w_cols.1) | copy-start | bytes 294916
  79.2 55.4 %copy-start.3 = (bf16[384,128]{1,0:T(8,128)(2,1)S(1)}, bf16[384,128]{1,0:T(8,128)(2,1)}, u32[]{:S(2)}) copy-start(bf16[384,128]{1,0:T(8,128)(2,1)} %w_rows.1) | copy-start | bytes 294916
  79.3 5.2 %collective-permute-start.1 = (bf16[864,128]{1,0:T(8,128)(2,1)S(1)}, bf16[864,128]{1,0:T(8,128)(2,1)S(1)}, u32[]{:S(2)}, u32[]{:S(2)}) collective-permute-start(bf16[864,128]{1,0:T(8,128)(2,1)S(1)} %dynamic-slice_convert_fusion), channel_id=1, source_target_pairs={{0,1},{1,0},{2,3},{3,2},{4,5},{5,4},{6,7},{7,6},{8,9},{9,8},{10,11... | collective-permute-start | bytes 663560 | tf_op jit(solution)/shard_map/ppermute | solution.py:235
  80.3 4.2 %collective-permute-start.2 = (bf16[96,128]{1,0:T(8,128)(2,1)S(1)}, bf16[96,128]{1,0:T(8,128)(2,1)S(1)}, u32[]{:S(2)}, u32[]{:S(2)}) collective-permute-start(bf16[96,128]{1,0:T(8,128)(2,1)S(1)} %convert_element_type.37), channel_id=1, source_target_pairs={{0,4},{1,5},{2,20},{3,21},{4,36},{5,37},{6,52},{7,53},{8,68},{9,69... | collective-permute-start | bytes 73736 | tf_op jit(solution)/shard_map/ppermute | solution.py:315
  84.7 3.9 %collective-permute-start.3 = (bf16[480,128]{1,0:T(8,128)(2,1)S(1)}, bf16[480,128]{1,0:T(8,128)(2,1)S(1)}, u32[]{:S(2)}, u32[]{:S(2)}) collective-permute-start(bf16[480,128]{1,0:T(8,128)(2,1)S(1)} %dynamic-slice_convert_fusion.1), channel_id=1, source_target_pairs={{0,2},{1,3},{2,0},{3,1},{4,6},{5,7},{6,4},{7,5},{8,10},{9,11},{10,... | collective-permute-start | bytes 368648 | tf_op jit(solution)/shard_map/ppermute | solution.py:235
  88.7 3.0 %collective-permute-start.4 = (bf16[192,128]{1,0:T(8,128)(2,1)S(1)}, bf16[192,128]{1,0:T(8,128)(2,1)S(1)}, u32[]{:S(2)}, u32[]{:S(2)}) collective-permute-start(bf16[192,128]{1,0:T(8,128)(2,1)S(1)} %dynamic-slice_convert_fusion.2), channel_id=1, source_target_pairs={{0,16},{1,17},{2,18},{3,19},{4,20},{5,21},{6,22},{7,23},{8,24},{9,... | collective-permute-start | bytes 147464 | tf_op jit(solution)/shard_map/ppermute | solution.py:235
  91.7 5.3 %collective-permute-start.5 = (f32[288,128]{1,0:T(8,128)S(1)}, f32[288,128]{1,0:T(8,128)S(1)}, u32[]{:S(2)}, u32[]{:S(2)}) collective-permute-start(f32[288,128]{1,0:T(8,128)S(1)} %pad_maximum_fusion.4), channel_id=1, source_target_pairs={{0,6},{1,7},{2,4},{3,5},{4,2},{5,3},{6,0},{7,1},{8,14},{9,15},{10,... | collective-permute-start | bytes 442376 | tf_op jit(solution)/shard_map/ppermute | solution.py:235
  97.0 8.3 %collective-permute-start.6 = (f32[288,128]{1,0:T(8,128)S(1)}, f32[288,128]{1,0:T(8,128)S(1)}, u32[]{:S(2)}, u32[]{:S(2)}) collective-permute-start(f32[288,128]{1,0:T(8,128)S(1)} %fusion.8), channel_id=1, source_target_pairs={{0,8},{1,9},{2,10},{3,11},{4,12},{5,13},{6,14},{7,15},{8,0},{9,1},... | collective-permute-start | bytes 442376 | tf_op jit(solution)/shard_map/ppermute | solution.py:235
  105.4 4.8 %collective-permute-start.7 = (f32[192,128]{1,0:T(8,128)S(1)}, f32[192,128]{1,0:T(8,128)S(1)}, u32[]{:S(2)}, u32[]{:S(2)}) collective-permute-start(f32[192,128]{1,0:T(8,128)S(1)} %slice.85), channel_id=1, source_target_pairs={{0,48},{1,49},{2,50},{3,51},{4,52},{5,53},{6,54},{7,55},{8,56},{9,... | collective-permute-start | bytes 294920 | tf_op jit(solution)/shard_map/ppermute | solution.py:235
  110.2 3.8 %collective-permute-start.8 = (f32[192,128]{1,0:T(8,128)S(1)}, f32[192,128]{1,0:T(8,128)S(1)}, u32[]{:S(2)}, u32[]{:S(2)}) collective-permute-start(f32[192,128]{1,0:T(8,128)S(1)} %slice_add_fusion), channel_id=1, source_target_pairs={{0,64},{1,65},{2,66},{3,67},{4,68},{5,69},{6,70},{7,71},{8,72},{9,... | collective-permute-start | bytes 294920 | tf_op jit(solution)/shard_map/ppermute | solution.py:235
  114.0 3.0 %collective-permute-start.9 = (bf16[192,128]{1,0:T(8,128)(2,1)S(1)}, bf16[192,128]{1,0:T(8,128)(2,1)S(1)}, u32[]{:S(2)}, u32[]{:S(2)}) collective-permute-start(bf16[192,128]{1,0:T(8,128)(2,1)S(1)} %add_convert_fusion), channel_id=1, source_target_pairs={{0,16},{1,17},{2,18},{3,19},{4,20},{5,21},{6,22},{7,23},{8,24},{9,... | collective-permute-start | bytes 147464 | tf_op jit(solution)/shard_map/ppermute | solution.py:235
  117.1 4.1 %collective-permute-start.10 = (bf16[480,128]{1,0:T(8,128)(2,1)S(1)}, bf16[480,128]{1,0:T(8,128)(2,1)S(1)}, u32[]{:S(2)}, u32[]{:S(2)}) collective-permute-start(bf16[480,128]{1,0:T(8,128)(2,1)S(1)} %pad_maximum_fusion.5), channel_id=1, source_target_pairs={{0,2},{1,3},{2,0},{3,1},{4,6},{5,7},{6,4},{7,5},{8,10},{9,11},{10,... | collective-permute-start | bytes 368648 | tf_op jit(solution)/shard_map/ppermute | solution.py:235
  121.2 10.8 %collective-permute-start.11 = (bf16[960,128]{1,0:T(8,128)(2,1)S(1)}, bf16[960,128]{1,0:T(8,128)(2,1)S(1)}, u32[]{:S(2)}, u32[]{:S(2)}) collective-permute-start(bf16[960,128]{1,0:T(8,128)(2,1)S(1)} %pad_maximum_fusion.3), channel_id=1, source_target_pairs={{0,1},{1,0},{2,3},{3,2},{4,5},{5,4},{6,7},{7,6},{8,9},{9,8},{10,11... | collective-permute-start | bytes 737288 | tf_op jit(solution)/shard_map/ppermute | solution.py:235

commit v2 on v1

v2 whole, which is shorter than its diff:
```python
import jax
import jax.numpy as jnp
from jax import lax
from jax.experimental import pallas as pl
from jax.experimental.pallas import tpu as pltpu
from jax.sharding import PartitionSpec as P

RBINS = 66
SLOT = 72
HOT = 2 * SLOT
NCHAIN = 8
PADDED = 1536
BOTH = ("row", "col")
ROWS = 48
GROUP = 24

BF = jnp.bfloat16
F32 = jnp.float32


UNITS = "mmm"
LAG = 2


def dot(left, right, dims=((1,), (0,))):
    return lax.dot_general(left, right, (dims, ((), ())), preferred_element_type=F32)


def split_dot(left, right):
    high = right.astype(BF)
    low = (right - high.astype(F32)).astype(BF)
    return dot(left, high, ((0,), (0,))) + dot(left, low, ((0,), (0,)))


def pair_kernel(
    chain_ids,
    bins,
    cot_ab,
    cot_z,
    single_rows,
    single_cols,
    chain_right,
    w_rows,
    w_cols,
    rel_table,
    gain_ref,
    bias_ref,
    w_in,
    sums,
    row_sums,
    col_sums,
    table,
    chain_hot,
    w_fwd,
    w_back,
    averager,
    proj_rows,
    base,
    col_acc,
    gw_acc,
    table_acc,
    gain_acc,
    bias_acc,
):
    step = pl.program_id(0)
    first_row = (lax.axis_index("row") * pl.num_programs(0) + step) * ROWS
    width = cot_z.shape[1]
    channels = cot_z.shape[2]
    hidden = channels
    gain = gain_ref[...]
    bias = bias_ref[...]

    @pl.when(step == 0)
    def _():
        wide = w_in[...].astype(F32)
        lane = lax.broadcasted_iota(jnp.int32, wide.shape, 1)
        is_gate = (lane // hidden) % 2 == 0
        w_fwd[...] = jnp.where(is_gate, wide * 0.5, wide).astype(BF)
        back = jnp.transpose(wide * jnp.where(is_gate, 0.25, 0.5))
        scaled = back * gain
        w_back[:, :channels] = (scaled - jnp.mean(scaled, axis=1, keepdims=True)).astype(BF)
        w_back[:, channels:] = back.astype(BF)
        averager[...] = jnp.full((channels, channels), 1.0 / channels, BF)
        proj_rows[...] = dot(single_rows[...], w_rows[...])
        cols = dot(single_cols[...], w_cols[...])
        known = rel_table[...].astype(F32)
        gap = jnp.zeros((SLOT - RBINS, channels), F32)
        table[...] = jnp.concatenate(
            [known[:RBINS], gap, known[RBINS : 2 * RBINS], gap], axis=0
        ).astype(BF)
        lane = lax.broadcasted_iota(jnp.int32, (width, channels), 1)
        right = chain_right[...]
        is_chain = (lane == right) | (lane == right + NCHAIN)
        chain_hot[...] = jnp.where(is_chain, 1.0, 0.0).astype(BF)
        offsets = known[2 * RBINS : 2 * RBINS + 5]
        same = known[2 * RBINS + 5 :]
        nothing = jnp.zeros((1, channels), F32)
        rest = jnp.zeros((channels - 2 * NCHAIN, channels), F32)
        for chain in range(NCHAIN):
            entries = []
            for other in range(NCHAIN):
                place = min(max(chain - other + 2, 0), 4)
                entries.append(offsets[place : place + 1])
            entries += [same if other == chain else nothing for other in range(NCHAIN)]
            mixed = jnp.concatenate(entries + [rest], axis=0).astype(BF)
            base[chain] = cols + dot(chain_hot[...], mixed)
        col_acc[...] = jnp.zeros_like(col_acc)
        gw_acc[...] = jnp.zeros_like(gw_acc)
        table_acc[...] = jnp.zeros_like(table_acc)
        gain_acc[...] = jnp.zeros_like(gain_acc)
        bias_acc[...] = jnp.zeros_like(bias_acc)

    pairs = GROUP * width
    bin_ids = lax.broadcasted_iota(jnp.int32, (SLOT, pairs), 0)
    proj_block = proj_rows[pl.ds(pl.multiple_of(step * ROWS, ROWS), ROWS), :]
    ones = averager[...]
    count = ROWS // GROUP
    state = [{} for _ in range(count)]
    row_list = [None] * ROWS

    def average(value, unit):
        if unit == "x":
            return jnp.mean(value, axis=1, keepdims=True)
        return dot(value.astype(BF), ones)

    def features(now, at):
        span = slice(at * width, at * width + pairs)
        both = bins[0, 0:1, span]
        res_hot = jnp.where(bin_ids == (both & 127), 1.0, 0.0)
        tok_hot = jnp.where(bin_ids == (both >> 7), 1.0, 0.0)
        now["hot"] = jnp.concatenate([res_hot, tok_hot], axis=0).astype(BF)
        now["relative"] = dot(now["hot"], table[...], ((0,), (0,))).reshape(GROUP, width, channels)

    def initial(now, at):
        chains = [chain_ids[first_row + at + k] for k in range(GROUP)]
        now["chains"] = chains
        pair = jnp.concatenate(
            [
                now["relative"][k] + base[chains[k]] + proj_block[at + k : at + k + 1, :]
                for k in range(GROUP)
            ],
            axis=0,
        ).astype(BF)
        wide = pair.astype(F32)
        now["centred"] = wide - (average(wide, "x") if UNITS[0] == "x" else dot(pair, ones))

    def norm(now, at):
        centred = now["centred"]
        variance = average(centred * centred, UNITS[1])
        now["inv_std"] = lax.rsqrt(variance + 1e-05)
        now["standard"] = centred * now["inv_std"]
        now["normed"] = (now["standard"] * gain + bias).astype(BF)

    def gates(now, at):
        projected = dot(now["normed"], w_fwd[...])
        parts = []
        for edge in range(2):
            begin = 2 * hidden * edge
            tanh = jnp.tanh(projected[:, begin : begin + hidden])
            value = projected[:, begin + hidden : begin + 2 * hidden]
            cot = cot_ab[at : at + GROUP, :, edge * hidden : (edge + 1) * hidden]
            cot = cot.reshape(pairs, hidden).astype(F32)
            double = cot + cot * tanh
            quad = double * value
            parts.append((quad - quad * tanh).astype(BF))
            parts.append(double.astype(BF))
        now["proj_grad"] = jnp.concatenate(parts, axis=1)

    def weights(now, at):
        gw_acc[...] += dot(now["normed"], now["proj_grad"], ((0,), (0,)))
        back = dot(now["proj_grad"], w_back[...])
        standard = now["standard"]
        normed_grad = back[:, channels:]
        product = normed_grad * standard
        gain_acc[...] += jnp.sum(product.reshape(pairs // 8, 8, channels), axis=0)
        bias_acc[...] += jnp.sum(normed_grad.reshape(pairs // 8, 8, channels), axis=0)
        now["scaled"] = back[:, :channels]
        now["slope"] = average(now["scaled"] * standard, UNITS[2])

    def finish(now, at):
        residual = cot_z[at : at + GROUP].reshape(pairs, channels).astype(F32)
        pair_grad = residual + now["inv_std"] * (now["scaled"] - now["standard"] * now["slope"])
        table_acc[...] += dot(now["hot"], pair_grad.astype(BF))
        grid = pair_grad.reshape(GROUP, width, channels)
        for k in range(GROUP):
            col_acc[now["chains"][k]] += grid[k]
            row_list[at + k] = jnp.sum(grid[k], axis=0, keepdims=True)

    stages = [features, initial, norm, gates, weights, finish]
    for tick in range(count * LAG + len(stages)):
        for group in range(count):
            stage = tick - group * LAG
            if 0 <= stage < len(stages):
                stages[stage](state[group], group * GROUP)
    row_sums[pl.ds(pl.multiple_of(step * ROWS, ROWS), ROWS), :] = jnp.concatenate(row_list, axis=0)

    @pl.when(step == pl.num_programs(0) - 1)
    def _():
        for part in range(4):
            scale = 0.25 if part % 2 == 0 else 0.5
            block = gw_acc[:, part * hidden : (part + 1) * hidden]
            sums[part * channels : (part + 1) * channels, :] = block * scale
        at = 4 * channels
        sums[at : at + HOT, :] = table_acc[...]
        total = jnp.zeros((width, channels), F32)
        places = [jnp.zeros((1, channels), F32) for _ in range(6)]
        for chain in range(NCHAIN):
            value = col_acc[chain]
            total = total + value
            by_chain = split_dot(chain_hot[...], value)
            for other in range(NCHAIN):
                place = min(max(chain - other + 2, 0), 4)
                places[place] = places[place] + by_chain[other : other + 1]
            places[5] = places[5] + by_chain[chain : chain + 1]
        col_sums[...] = total
        for place in range(6):
            sums[at + RBINS + place : at + RBINS + place + 1, :] = places[place]
        spare = at + SLOT + RBINS
        sums[spare : spare + 1, :] = jnp.sum(gain_acc[...], axis=0, keepdims=True)
        sums[spare + 1 : spare + 2, :] = jnp.sum(bias_acc[...], axis=0, keepdims=True)
        at = at + HOT
        depth = single_rows.shape[1]
        sums[at : at + depth, :] = split_dot(single_rows[...], row_sums[...])
        at = at + depth
        sums[at : at + depth, :] = split_dot(single_cols[...], total)
        at = at + depth
        sums[at:, :] = jnp.zeros((sums.shape[0] - at, channels), F32)


def pair_work(chain_ids, bins, cot_ab, cot_z, *rest):
    row_tok, col_tok, channels = cot_z.shape
    steps = row_tok // ROWS

    def whole(array):
        return pl.BlockSpec(array.shape, lambda i: (0,) * array.ndim)

    results = [
        jax.ShapeDtypeStruct((PADDED, channels), F32),
        jax.ShapeDtypeStruct((row_tok, channels), F32),
        jax.ShapeDtypeStruct((col_tok, channels), F32),
    ]
    return pl.pallas_call(
        pair_kernel,
        grid=(steps,),
        in_specs=[
            pl.BlockSpec(memory_space=pltpu.SMEM),
            pl.BlockSpec((1, 1, ROWS * col_tok), lambda i: (i, 0, 0)),
            pl.BlockSpec((ROWS, col_tok, 2 * channels), lambda i: (i, 0, 0)),
            pl.BlockSpec((ROWS, col_tok, channels), lambda i: (i, 0, 0)),
        ]
        + [whole(array) for array in rest],
        out_specs=[whole(result) for result in results],
        out_shape=results,
        scratch_shapes=[
            pltpu.VMEM((HOT, channels), BF),
            pltpu.VMEM((col_tok, channels), BF),
            pltpu.VMEM((channels, 4 * channels), BF),
            pltpu.VMEM((4 * channels, 2 * channels), BF),
            pltpu.VMEM((channels, channels), BF),
            pltpu.VMEM((row_tok, channels), F32),
            pltpu.VMEM((NCHAIN, col_tok, channels), F32),
            pltpu.VMEM((NCHAIN, col_tok, channels), F32),
            pltpu.VMEM((channels, 4 * channels), F32),
            pltpu.VMEM((HOT, channels), F32),
            pltpu.VMEM((8, channels), F32),
            pltpu.VMEM((8, channels), F32),
        ],
        compiler_params=pltpu.CompilerParams(vmem_limit_bytes=50 * 1024 * 1024),
        cost_estimate=pl.CostEstimate(
            flops=9 * 10**9, bytes_accessed=15 * 10**6, transcendentals=7 * 10**6
        ),
    )(chain_ids, bins, cot_ab, cot_z, *rest)


def result_kernel(tokens, core, mine, theirs, w_rows, w_cols, *outs):
    grad_single, grad_w_rows, grad_w_cols, grad_table, grad_gain, grad_bias, grad_w_in = outs
    is_first = core[0] == 0
    channels = w_rows.shape[1]
    depth = w_rows.shape[0]
    quarter = PADDED // 4

    def fetch(low, high):
        first = jnp.where(is_first, mine[low:high], theirs[low:high])
        second = jnp.where(is_first, theirs[low:high], mine[low:high])
        return first, second

    def weights(low, high):
        pieces = []
        for part in range(4):
            begin, end = max(low - part * quarter, 0), min(high - part * quarter, quarter)
            if begin < end:
                shift = (part % 2) * (quarter + 2 * tokens)
                pieces.append(fetch(begin + shift, end + shift)[part // 2].astype(F32))
        return pieces[0] if len(pieces) == 1 else jnp.concatenate(pieces, axis=0)

    parts = []
    for kind in range(2):
        pieces = []
        for half in range(2):
            low = half * (quarter + 2 * tokens) + quarter + kind * tokens
            pieces.append(fetch(low, low + tokens))
        parts.append(jnp.concatenate([pieces[0][0], pieces[1][0], pieces[0][1], pieces[1][1]], axis=0))
    back = ((1,), (1,))
    grad_single[...] = dot(parts[0], w_rows[...], back) + dot(parts[1], w_cols[...], back)
    for part in range(4):
        at = part * channels
        grad_w_in[:, at : at + channels] = weights(at, at + channels)
    at = 4 * channels
    table = weights(at, at + HOT)
    grad_table[...] = jnp.concatenate(
        [table[:RBINS], table[SLOT : SLOT + RBINS], table[RBINS:SLOT]], axis=0
    )
    grad_gain[...] = table[SLOT + RBINS : SLOT + RBINS + 1]
    grad_bias[...] = table[SLOT + RBINS + 1 : SLOT + RBINS + 2]
    at = at + HOT
    grad_w_rows[...] = weights(at, at + depth)
    grad_w_cols[...] = weights(at + depth, at + 2 * depth)


def results(tokens, core, mine, theirs, w_rows, w_cols, row_tok):
    depth, channels = w_rows.shape
    shapes = [
        (row_tok, depth),
        (depth, channels),
        (depth, channels),
        (2 * RBINS + 6, channels),
        (1, channels),
        (1, channels),
        (channels, 4 * channels),
    ]

    def kernel(*refs):
        result_kernel(tokens, *refs)

    def whole(shape):
        return pl.BlockSpec(shape, lambda i: (0,) * len(shape))

    return pl.pallas_call(
        kernel,
        grid=(1,),
        in_specs=[pl.BlockSpec(memory_space=pltpu.SMEM)]
        + [whole(array.shape) for array in (mine, theirs, w_rows, w_cols)],
        out_specs=[whole(shape) for shape in shapes],
        out_shape=[jax.ShapeDtypeStruct(shape, F32) for shape in shapes],
        compiler_params=pltpu.CompilerParams(vmem_limit_bytes=30 * 1024 * 1024),
    )(core, mine, theirs, w_rows, w_cols)


def join_bins(res_bin, tok_bin):
    def kernel(res, tok, out):
        out[...] = res[...] + 128 * tok[...]

    return pl.pallas_call(
        kernel,
        out_shape=jax.ShapeDtypeStruct(res_bin.shape, res_bin.dtype),
        in_specs=[pl.BlockSpec(memory_space=pltpu.VMEM)] * 2,
        out_specs=pl.BlockSpec(memory_space=pltpu.VMEM),
        cost_estimate=pl.CostEstimate(flops=10**10, bytes_accessed=10**6, transcendentals=0),
    )(res_bin, tok_bin)


def turned(row, col):
    z_lo, x = row // 4, row % 4
    z_hi, y, core = col // 8, col // 2 % 4, col % 2
    return z_hi * 4 + y, z_lo * 8 + (x + 2) % 4 * 2 + core


def turn_pairs():
    pairs = []
    for row in range(8):
        for col in range(16):
            to_row, to_col = turned(row, col)
            pairs.append((row * 16 + col, to_row * 16 + to_col))
    return pairs


def swap(value, mask):
    return lax.ppermute(value, BOTH, [(at, at ^ mask) for at in range(128)])


def pick(value, place):
    half = value.shape[0] // 2
    return lax.dynamic_slice_in_dim(value, place * half, half, 0)


def halve(value, place, mask):
    got = swap(pick(value, 1 - place).astype(BF), mask)
    return pick(value, place) + got.astype(F32)


def both_sum(value, mask):
    return value + swap(value, mask)


def double(value, place, mask):
    got = swap(value, mask)
    first = jnp.where(place == 0, value, got)
    second = jnp.where(place == 0, got, value)
    return jnp.concatenate([first, second], axis=0)


def per_device(
    single,
    res_bin,
    tok_bin,
    chain_ids,
    w_rows,
    w_cols,
    rel_table,
    ln_gain,
    ln_bias,
    w_in,
    cot_ab,
    cot_z,
):
    row_tok, col_tok = res_bin.shape
    channels = w_rows.shape[1]
    row_at = lax.axis_index("row")
    col_at = lax.axis_index("col")
    core = col_at % 2
    y_at = col_at // 2 % 4
    y_half = (y_at % 2) ^ (y_at // 2)
    x_at = row_at % 4
    x_half = (x_at % 2) ^ (x_at // 2)
    turn = turn_pairs()

    single_cols = lax.ppermute(pick(single, core), BOTH, [(to, at) for at, to in turn])
    chain_right = lax.dynamic_slice_in_dim(chain_ids, col_at * col_tok, col_tok, 0)
    chain_right = jnp.broadcast_to(chain_right[:, None], (col_tok, channels))
    bins = join_bins(res_bin, tok_bin).reshape(row_tok // ROWS, 1, ROWS * col_tok)
    sums, row_sums, col_sums = pair_work(
        chain_ids,
        bins,
        cot_ab,
        cot_z,
        single,
        single_cols,
        chain_right,
        w_rows,
        w_cols,
        rel_table,
        ln_gain[None, :],
        ln_bias[None, :],
        w_in,
    )
    cols = lax.ppermute(col_sums.astype(BF), BOTH, turn).astype(F32)
    halves = jnp.concatenate(
        [
            sums.reshape(2, PADDED // 2, channels),
            row_sums.reshape(2, row_tok // 2, channels),
        ],
        axis=1,
    )
    held = halve(halves.reshape(PADDED + row_tok, channels), core, 1)
    weights, rows = held[: PADDED // 2], held[PADDED // 2 :]
    quarter = PADDED // 4
    tok = row_tok // 4
    mixed = jnp.concatenate(
        [
            weights.reshape(2, quarter, channels),
            rows.reshape(2, tok, channels),
            cols.reshape(2, tok, channels),
        ],
        axis=1,
    )
    held = halve(mixed.reshape(-1, channels), y_half, 2)
    weights, tokens = halve(held[:quarter], x_half, 16), held[quarter:]
    eighth = quarter // 2
    held = jnp.concatenate([weights, tokens], axis=0)
    held = both_sum(held, 6)
    held = both_sum(held, 8)
    weights, tokens = held[:eighth], held[eighth:]
    weights = both_sum(weights, 48)
    weights = both_sum(weights, 64)
    weights = double(weights.astype(BF), x_half, 16)
    done = jnp.concatenate([weights, tokens.astype(BF)], axis=0)
    done = double(done, y_half, 2)
    outs = results(tok, core.reshape(1), done, swap(done, 1), w_rows, w_cols, row_tok)
    grad_single, grad_w_rows, grad_w_cols, grad_table, grad_gain, grad_bias, grad_w_in = outs
    return (
        grad_single,
        grad_w_rows,
        grad_w_cols,
        grad_table,
        grad_gain.reshape(channels),
        grad_bias.reshape(channels),
        grad_w_in,
    )


def solution(mesh):
    in_specs = (
        P("row", None),
        P("row", "col"),
        P("row", "col"),
        P(),
        P(),
        P(),
        P(),
        P(),
        P(),
        P(),
        P("row", "col", None),
        P("row", "col", None),
    )
    out_specs = (P("row", None), P(), P(), P(), P(), P(), P())
    return jax.shard_map(
        per_device, mesh=mesh, in_specs=in_specs, out_specs=out_specs, check_vma=False
    )
```

time: 137 us -> 93.7 us (0.68)
  Pallas kernels: 63.7 us -> 32.4 us
  local copies, waits for them, and re-layouts: 13.4 us -> 2.28 us
  starting transfers between devices: 28.6 us -> 33.9 us
  waiting for transfers between devices: 27.1 us -> 23.6 us
    pallas_call x1, Pallas kernels: 63.7 us -> 29.6 us  [pair_work(): pl.pallas_call(pair_kernel, grid=(steps,), in_specs=[pl.BlockSpec(memory_...]
    unnamed x17 -> x16, local copies, waits for them, and re-layouts: 5.65 us -> 0.05 us
    pallas_call x0 -> x2, Pallas kernels: none -> 2.75 us  [the longest x1 1.59 us: join_bins(): pl.pallas_call(kernel, out_shape=jax.ShapeDtypeStruct(res_bin.shape, res_...]
    ppermute x10, starting transfers between devices: 24.6 us -> 27.2 us  [swap(): return lax.ppermute(value, BOTH, [(at, at ^ mask) for at in range(128)])]
    ppermute x1, starting transfers between devices: 0.43 us -> 3.01 us  [per_device(): cols = lax.ppermute(col_sums.astype(BF), BOTH, turn).astype(F32)]
    ppermute x1, waiting for transfers between devices: 3.77 us -> 1.18 us  [per_device(): cols = lax.ppermute(col_sums.astype(BF), BOTH, turn).astype(F32)]
    slice x10 -> x2, local copies, waits for them, and re-layouts: 2.37 us -> 0.03 us  [per_device(): weights, rows = (held[:PADDED // 2], held[PADDED // 2:])]
    another operation x2 -> x0, local copies, waits for them, and re-layouts: 2.09 us -> none  [per_device(): jnp.stack([res_bin.reshape(steps, ROWS * col_tok), tok_bin.reshape(steps,...]
  transfers between devices with their start and end apart: 12 -> 12, of which waited for: 10 -> 10; matrix products, arithmetic and copies ran while one was open for 4% -> 1% of each run, Pallas kernels for 0% -> 2%
where the time goes in v2:
time: 93.7 us; the launch traced here: 93.5 us
  starting transfers between devices  33.9 us (36%)
  Pallas kernels  32.4 us (35%)
  waiting for transfers between devices  23.6 us (25%)
  local copies, waits for them, and re-layouts  2.28 us (2%)
  between operations  0.96 us (1%)
    pallas_call x1, Pallas kernels, pair_work(): pl.pallas_call(pair_kernel, grid=(steps,), in_specs=[pl.BlockSpec(memory_...  29.6 us
    ppermute x10, starting transfers between devices, swap(): return lax.ppermute(value, BOTH, [(at, at ^ mask) for at in range(128)])  27.2 us
    ppermute x10, waiting for transfers between devices, swap(): return lax.ppermute(value, BOTH, [(at, at ^ mask) for at in range(128)])  22.4 us
    ppermute x1, starting transfers between devices, per_device(): lax.ppermute(pick(single, core), BOTH, [(to, at) for at, to in turn])  3.64 us
    ppermute x1, starting transfers between devices, per_device(): cols = lax.ppermute(col_sums.astype(BF), BOTH, turn).astype(F32)  3.01 us
  transfers between devices with their start and end apart: 12, of which 10 were waited for; matrix products, arithmetic and copies ran while one was open for 1% of the time, Pallas kernels for 2%

profile of v2, /device:TPU:1, one launch (start us, length us, event | category | flops | bytes accessed | tf_op | source)
XLA Modules:
  0.0 93.5 jit_solution(14512286121097189323)
XLA Ops:
  0.7 0.9 constant_dynamic-slice_fusion
  1.5 0.0 copy-start.5
  1.6 0.0 copy-start
  1.6 0.0 copy-start.1
  1.6 0.0 copy-start.2
  1.6 0.0 copy-start.3
  1.6 0.0 copy-start.4
  1.6 0.0 copy-start.6
  1.6 0.0 copy-start.7
  1.6 3.6 %collective-permute-start = (bf16[96,384]{1,0:T(8,128)(2,1)S(1)}, bf16[96,384]{1,0:T(8,128)(2,1)S(1)}, u32[]{:S(2)}, u32[]{:S(2)}) collective-permute-start(bf16[96,384]{1,0:T(8,128)(2,1)S(1)} %constant_dynamic-slice_fusion), channel_id=1, source_target_pairs={{4,0},{5,1},{20,2},{21,3},{36,4},{37,5},{52,6},{53,7},{68,8},{69,9... | collective-permute-start | bytes 221192 | tf_op jit(solution)/shard_map/ppermute | solution.py:427
  5.3 1.6 %shard_map.171 = s32[192,96]{1,0:T(8,128)} custom-call(s32[192,96]{1,0:T(8,128)} %res.1, s32[192,96]{1,0:T(8,128)} %tok.1), custom_call_target="tpu_custom_call" | custom-call | flops 10000000000 | bytes 1000000 | tf_op jit(solution)/shard_map/pallas_call | solution.py:353
  6.9 1.0 %reshape.52.bins = s32[4,1,4608]{2,1,0:T(1,128)S(1)} reshape(s32[192,96]{1,0:T(8,128)} %shard_map.171) | data formatting | bytes 147456 | tf_op jit(solution)/shard_map/reshape | solution.py:430
  7.9 0.0 copy-done.5
  7.9 0.1 dynamic_slice.25
  8.0 0.0 collective-permute-done.single_cols
  8.0 0.1 broadcast_in_dim.12.chain_right
  8.1 0.0 copy-done
  8.1 0.0 copy-done.1
  8.1 0.0 copy-done.2
  8.1 0.0 copy-done.3
  8.1 0.0 copy-done.4
  8.1 0.0 copy-done.6
  8.2 0.0 copy-done.7
  8.2 29.6 %shard_map.172 = (f32[1536,128]{1,0:T(8,128)S(1)}, f32[192,128]{1,0:T(8,128)S(1)}, f32[96,128]{1,0:T(8,128)S(1)}) custom-call(s32[1536]{0:T(1024)S(1)} %copy-done.5, s32[4,1,4608]{2,1,0:T(1,128)S(1)} %reshape.52.bins, bf16[192,96,256]{2,1,0:T(8,128)(2,1)} %cot_ab.1, bf16[192,96,128]{2,1,0:T(8,128)(2,1)} %cot_z.1, bf16[192,384]{1,0:T(8,128)(2,1)S(1)} %copy-done.2, ...), custom_call_target="tpu_custom_call" | custom-call | flops 8999999488 | bytes 15000000 | tf_op jit(solution)/shard_map/pallas_call | solution.py:242
  37.8 0.1 pad_maximum_fusion
  37.9 1.0 %collective-permute-start.1 = (bf16[864,128]{1,0:T(8,128)(2,1)S(1)}, bf16[864,128]{1,0:T(8,128)(2,1)S(1)}, u32[]{:S(2)}, u32[]{:S(2)}) collective-permute-start(bf16[864,128]{1,0:T(8,128)(2,1)S(1)} %dynamic-slice_convert_fusion), channel_id=1, source_target_pairs={{0,1},{1,0},{2,3},{3,2},{4,5},{5,4},{6,7},{7,6},{8,9},{9,8},{10,11... | collective-permute-start | bytes 663560 | tf_op jit(solution)/shard_map/ppermute | solution.py:378
  38.9 3.0 %collective-permute-start.2 = (bf16[96,128]{1,0:T(8,128)(2,1)S(1)}, bf16[96,128]{1,0:T(8,128)(2,1)S(1)}, u32[]{:S(2)}, u32[]{:S(2)}) collective-permute-start(bf16[96,128]{1,0:T(8,128)(2,1)S(1)} %convert_element_type.28), channel_id=1, source_target_pairs={{0,4},{1,5},{2,20},{3,21},{4,36},{5,37},{6,52},{7,53},{8,68},{9,69... | collective-permute-start | bytes 73736 | tf_op jit(solution)/shard_map/ppermute | solution.py:446
  42.0 1.2 %collective-permute-done.2 = bf16[96,128]{1,0:T(8,128)(2,1)S(1)} collective-permute-done((bf16[96,128]{1,0:T(8,128)(2,1)S(1)}, bf16[96,128]{1,0:T(8,128)(2,1)S(1)}, u32[]{:S(2)}, u32[]{:S(2)}) %collective-permute-start.2) | collective-permute-done | bytes 24608 | tf_op jit(solution)/shard_map/ppermute | solution.py:446
  43.1 0.0 collective-permute-done.1
  43.1 0.1 convert_add_fusion
  43.3 2.7 %collective-permute-start.3 = (bf16[480,128]{1,0:T(8,128)(2,1)S(1)}, bf16[480,128]{1,0:T(8,128)(2,1)S(1)}, u32[]{:S(2)}, u32[]{:S(2)}) collective-permute-start(bf16[480,128]{1,0:T(8,128)(2,1)S(1)} %dynamic-slice_convert_fusion.1), channel_id=1, source_target_pairs={{0,2},{1,3},{2,0},{3,1},{4,6},{5,7},{6,4},{7,5},{8,10},{9,11},{10,... | collective-permute-start | bytes 368648 | tf_op jit(solution)/shard_map/ppermute | solution.py:378
  46.0 2.7 %collective-permute-done.3 = bf16[480,128]{1,0:T(8,128)(2,1)S(1)} collective-permute-done((bf16[480,128]{1,0:T(8,128)(2,1)S(1)}, bf16[480,128]{1,0:T(8,128)(2,1)S(1)}, u32[]{:S(2)}, u32[]{:S(2)}) %collective-permute-start.3) | collective-permute-done | bytes 122912 | tf_op jit(solution)/shard_map/ppermute | solution.py:378
  48.8 0.7 collective-permute-start.4
  49.5 2.3 %collective-permute-done.4 = bf16[192,128]{1,0:T(8,128)(2,1)S(1)} collective-permute-done((bf16[192,128]{1,0:T(8,128)(2,1)S(1)}, bf16[192,128]{1,0:T(8,128)(2,1)S(1)}, u32[]{:S(2)}, u32[]{:S(2)}) %collective-permute-start.4) | collective-permute-done | bytes 49184 | tf_op jit(solution)/shard_map/ppermute | solution.py:378
  51.8 3.3 %collective-permute-start.5 = (f32[288,128]{1,0:T(8,128)S(1)}, f32[288,128]{1,0:T(8,128)S(1)}, u32[]{:S(2)}, u32[]{:S(2)}) collective-permute-start(f32[288,128]{1,0:T(8,128)S(1)} %pad_maximum_fusion.3), channel_id=1, source_target_pairs={{0,6},{1,7},{2,4},{3,5},{4,2},{5,3},{6,0},{7,1},{8,14},{9,15},{10,... | collective-permute-start | bytes 442376 | tf_op jit(solution)/shard_map/ppermute | solution.py:378
  55.2 2.5 %collective-permute-done.5 = f32[288,128]{1,0:T(8,128)S(1)} collective-permute-done((f32[288,128]{1,0:T(8,128)S(1)}, f32[288,128]{1,0:T(8,128)S(1)}, u32[]{:S(2)}, u32[]{:S(2)}) %collective-permute-start.5) | collective-permute-done | bytes 147488 | tf_op jit(solution)/shard_map/ppermute | solution.py:378
  57.7 5.5 %collective-permute-start.6 = (f32[288,128]{1,0:T(8,128)S(1)}, f32[288,128]{1,0:T(8,128)S(1)}, u32[]{:S(2)}, u32[]{:S(2)}) collective-permute-start(f32[288,128]{1,0:T(8,128)S(1)} %fusion), channel_id=1, source_target_pairs={{0,8},{1,9},{2,10},{3,11},{4,12},{5,13},{6,14},{7,15},{8,0},{9,1},... | collective-permute-start | bytes 442376 | tf_op jit(solution)/shard_map/ppermute | solution.py:378
  63.2 2.5 %collective-permute-done.6 = f32[288,128]{1,0:T(8,128)S(1)} collective-permute-done((f32[288,128]{1,0:T(8,128)S(1)}, f32[288,128]{1,0:T(8,128)S(1)}, u32[]{:S(2)}, u32[]{:S(2)}) %collective-permute-start.6) | collective-permute-done | bytes 147488 | tf_op jit(solution)/shard_map/ppermute | solution.py:378
  65.8 2.9 %collective-permute-start.7 = (f32[192,128]{1,0:T(8,128)S(1)}, f32[192,128]{1,0:T(8,128)S(1)}, u32[]{:S(2)}, u32[]{:S(2)}) collective-permute-start(f32[192,128]{1,0:T(8,128)S(1)} %slice.29), channel_id=1, source_target_pairs={{0,48},{1,49},{2,50},{3,51},{4,52},{5,53},{6,54},{7,55},{8,56},{9,... | collective-permute-start | bytes 294920 | tf_op jit(solution)/shard_map/ppermute | solution.py:378
  68.7 2.0 %collective-permute-done.7 = f32[192,128]{1,0:T(8,128)S(1)} collective-permute-done((f32[192,128]{1,0:T(8,128)S(1)}, f32[192,128]{1,0:T(8,128)S(1)}, u32[]{:S(2)}, u32[]{:S(2)}) %collective-permute-start.7) | collective-permute-done | bytes 98336 | tf_op jit(solution)/shard_map/ppermute | solution.py:378
  70.7 1.3 %collective-permute-start.8 = (f32[192,128]{1,0:T(8,128)S(1)}, f32[192,128]{1,0:T(8,128)S(1)}, u32[]{:S(2)}, u32[]{:S(2)}) collective-permute-start(f32[192,128]{1,0:T(8,128)S(1)} %slice_add_fusion), channel_id=1, source_target_pairs={{0,64},{1,65},{2,66},{3,67},{4,68},{5,69},{6,70},{7,71},{8,72},{9,... | collective-permute-start | bytes 294920 | tf_op jit(solution)/shard_map/ppermute | solution.py:378
  72.0 2.3 %collective-permute-done.8 = f32[192,128]{1,0:T(8,128)S(1)} collective-permute-done((f32[192,128]{1,0:T(8,128)S(1)}, f32[192,128]{1,0:T(8,128)S(1)}, u32[]{:S(2)}, u32[]{:S(2)}) %collective-permute-start.8) | collective-permute-done | bytes 98336 | tf_op jit(solution)/shard_map/ppermute | solution.py:378
  74.3 0.1 collective-permute-start.9
  74.4 2.9 %collective-permute-done.9 = bf16[192,128]{1,0:T(8,128)(2,1)S(1)} collective-permute-done((bf16[192,128]{1,0:T(8,128)(2,1)S(1)}, bf16[192,128]{1,0:T(8,128)(2,1)S(1)}, u32[]{:S(2)}, u32[]{:S(2)}) %collective-permute-start.9) | collective-permute-done | bytes 49184 | tf_op jit(solution)/shard_map/ppermute | solution.py:378
  77.3 0.1 collective-permute-start.10
  77.4 4.0 %collective-permute-done.10 = bf16[480,128]{1,0:T(8,128)(2,1)S(1)} collective-permute-done((bf16[480,128]{1,0:T(8,128)(2,1)S(1)}, bf16[480,128]{1,0:T(8,128)(2,1)S(1)}, u32[]{:S(2)}, u32[]{:S(2)}) %collective-permute-start.10) | collective-permute-done | bytes 122912 | tf_op jit(solution)/shard_map/ppermute | solution.py:378
  81.4 0.1 broadcast_select_fusion.1
  81.5 9.7 %collective-permute-start.11 = (bf16[960,128]{1,0:T(8,128)(2,1)S(1)}, bf16[960,128]{1,0:T(8,128)(2,1)S(1)}, u32[]{:S(2)}, u32[]{:S(2)}) collective-permute-start(bf16[960,128]{1,0:T(8,128)(2,1)S(1)} %pad_maximum_fusion.2.refs_1_), channel_id=1, source_target_pairs={{0,1},{1,0},{2,3},{3,2},{4,5},{5,4},{6,7},{7,6},{8,9},{9,8},{10,11... | collective-permute-start | bytes 737288 | tf_op jit(solution)/shard_map/ppermute | solution.py:378
  91.2 1.1 %collective-permute-done.11.refs_2_ = bf16[960,128]{1,0:T(8,128)(2,1)S(1)} collective-permute-done((bf16[960,128]{1,0:T(8,128)(2,1)S(1)}, bf16[960,128]{1,0:T(8,128)(2,1)S(1)}, u32[]{:S(2)}, u32[]{:S(2)}) %collective-permute-start.11) | collective-permute-done | bytes 245792 | tf_op jit(solution)/shard_map/ppermute | solution.py:378
  92.3 1.2 %shard_map.173 = (f32[192,384]{1,0:T(8,128)}, f32[384,128]{1,0:T(8,128)}, f32[384,128]{1,0:T(8,128)}, f32[138,128]{1,0:T(8,128)}, f32[1,128]{1,0:T(1,128)}, /*index=5*/f32[1,128]{1,0:T(1,128)}, f32[128,512]{1,0:T(8,128)}) custom-call(s32[1]{0:T(128)} %bitcast.refs_0_, bf16[960,128]{1,0:T(8,128)(2,1)S(1)} %pad_maximum_fusion.2.refs_1_, ...), custom_call_target="tpu_custom_call" | custom-call | tf_op jit(solution)/shard_map/pallas_call | solution.py:338
  (22 shorter events, 0.3 us)
Async XLA Ops:
  1.5 6.4 %copy-start.5 = (s32[1536]{0:T(1024)S(1)}, s32[1536]{0:T(1024)}, u32[]{:S(2)}) copy-start(s32[1536]{0:T(1024)} %chain_ids.1) | copy-start | bytes 18436
  1.6 6.5 %copy-start = (bf16[384,128]{1,0:T(8,128)(2,1)S(1)}, bf16[384,128]{1,0:T(8,128)(2,1)}, u32[]{:S(2)}) copy-start(bf16[384,128]{1,0:T(8,128)(2,1)} %refs_3_.1) | copy-start | bytes 294916
  1.6 6.5 %copy-start.1 = (bf16[384,128]{1,0:T(8,128)(2,1)S(1)}, bf16[384,128]{1,0:T(8,128)(2,1)}, u32[]{:S(2)}) copy-start(bf16[384,128]{1,0:T(8,128)(2,1)} %refs_4_.1) | copy-start | bytes 294916
  1.6 6.5 %copy-start.2 = (bf16[192,384]{1,0:T(8,128)(2,1)S(1)}, bf16[192,384]{1,0:T(8,128)(2,1)}, u32[]{:S(2)}) copy-start(bf16[192,384]{1,0:T(8,128)(2,1)} %single_rows.1) | copy-start | bytes 442372
  1.6 6.5 %copy-start.3 = (bf16[128,512]{1,0:T(8,128)(2,1)S(1)}, bf16[128,512]{1,0:T(8,128)(2,1)}, u32[]{:S(2)}) copy-start(bf16[128,512]{1,0:T(8,128)(2,1)} %w_in.1) | copy-start | bytes 393220
  1.6 6.5 %copy-start.4 = (bf16[138,128]{1,0:T(8,128)(2,1)S(1)}, bf16[138,128]{1,0:T(8,128)(2,1)}, u32[]{:S(2)}) copy-start(bf16[138,128]{1,0:T(8,128)(2,1)} %rel_table.1) | copy-start | bytes 105988
  1.6 6.5 %copy-start.6 = (f32[128]{0:T(128)S(1)}, f32[128]{0:T(128)}, u32[]{:S(2)}) copy-start(f32[128]{0:T(128)} %param.19) | copy-start | bytes 1540
  1.6 6.5 %copy-start.7 = (f32[128]{0:T(128)S(1)}, f32[128]{0:T(128)}, u32[]{:S(2)}) copy-start(f32[128]{0:T(128)} %param.20) | copy-start | bytes 1540
  1.6 6.4 %collective-permute-start = (bf16[96,384]{1,0:T(8,128)(2,1)S(1)}, bf16[96,384]{1,0:T(8,128)(2,1)S(1)}, u32[]{:S(2)}, u32[]{:S(2)}) collective-permute-start(bf16[96,384]{1,0:T(8,128)(2,1)S(1)} %constant_dynamic-slice_fusion), channel_id=1, source_target_pairs={{4,0},{5,1},{20,2},{21,3},{36,4},{37,5},{52,6},{53,7},{68,8},{69,9... | collective-permute-start | bytes 221192 | tf_op jit(solution)/shard_map/ppermute | solution.py:427
  37.9 5.2 %collective-permute-start.1 = (bf16[864,128]{1,0:T(8,128)(2,1)S(1)}, bf16[864,128]{1,0:T(8,128)(2,1)S(1)}, u32[]{:S(2)}, u32[]{:S(2)}) collective-permute-start(bf16[864,128]{1,0:T(8,128)(2,1)S(1)} %dynamic-slice_convert_fusion), channel_id=1, source_target_pairs={{0,1},{1,0},{2,3},{3,2},{4,5},{5,4},{6,7},{7,6},{8,9},{9,8},{10,11... | collective-permute-start | bytes 663560 | tf_op jit(solution)/shard_map/ppermute | solution.py:378
  38.9 4.2 %collective-permute-start.2 = (bf16[96,128]{1,0:T(8,128)(2,1)S(1)}, bf16[96,128]{1,0:T(8,128)(2,1)S(1)}, u32[]{:S(2)}, u32[]{:S(2)}) collective-permute-start(bf16[96,128]{1,0:T(8,128)(2,1)S(1)} %convert_element_type.28), channel_id=1, source_target_pairs={{0,4},{1,5},{2,20},{3,21},{4,36},{5,37},{6,52},{7,53},{8,68},{9,69... | collective-permute-start | bytes 73736 | tf_op jit(solution)/shard_map/ppermute | solution.py:446
  43.3 5.4 %collective-permute-start.3 = (bf16[480,128]{1,0:T(8,128)(2,1)S(1)}, bf16[480,128]{1,0:T(8,128)(2,1)S(1)}, u32[]{:S(2)}, u32[]{:S(2)}) collective-permute-start(bf16[480,128]{1,0:T(8,128)(2,1)S(1)} %dynamic-slice_convert_fusion.1), channel_id=1, source_target_pairs={{0,2},{1,3},{2,0},{3,1},{4,6},{5,7},{6,4},{7,5},{8,10},{9,11},{10,... | collective-permute-start | bytes 368648 | tf_op jit(solution)/shard_map/ppermute | solution.py:378
  48.8 3.0 %collective-permute-start.4 = (bf16[192,128]{1,0:T(8,128)(2,1)S(1)}, bf16[192,128]{1,0:T(8,128)(2,1)S(1)}, u32[]{:S(2)}, u32[]{:S(2)}) collective-permute-start(bf16[192,128]{1,0:T(8,128)(2,1)S(1)} %dynamic-slice_convert_fusion.2), channel_id=1, source_target_pairs={{0,16},{1,17},{2,18},{3,19},{4,20},{5,21},{6,22},{7,23},{8,24},{9,... | collective-permute-start | bytes 147464 | tf_op jit(solution)/shard_map/ppermute | solution.py:378
  51.8 5.9 %collective-permute-start.5 = (f32[288,128]{1,0:T(8,128)S(1)}, f32[288,128]{1,0:T(8,128)S(1)}, u32[]{:S(2)}, u32[]{:S(2)}) collective-permute-start(f32[288,128]{1,0:T(8,128)S(1)} %pad_maximum_fusion.3), channel_id=1, source_target_pairs={{0,6},{1,7},{2,4},{3,5},{4,2},{5,3},{6,0},{7,1},{8,14},{9,15},{10,... | collective-permute-start | bytes 442376 | tf_op jit(solution)/shard_map/ppermute | solution.py:378
  57.7 8.0 %collective-permute-start.6 = (f32[288,128]{1,0:T(8,128)S(1)}, f32[288,128]{1,0:T(8,128)S(1)}, u32[]{:S(2)}, u32[]{:S(2)}) collective-permute-start(f32[288,128]{1,0:T(8,128)S(1)} %fusion), channel_id=1, source_target_pairs={{0,8},{1,9},{2,10},{3,11},{4,12},{5,13},{6,14},{7,15},{8,0},{9,1},... | collective-permute-start | bytes 442376 | tf_op jit(solution)/shard_map/ppermute | solution.py:378
  65.8 4.9 %collective-permute-start.7 = (f32[192,128]{1,0:T(8,128)S(1)}, f32[192,128]{1,0:T(8,128)S(1)}, u32[]{:S(2)}, u32[]{:S(2)}) collective-permute-start(f32[192,128]{1,0:T(8,128)S(1)} %slice.29), channel_id=1, source_target_pairs={{0,48},{1,49},{2,50},{3,51},{4,52},{5,53},{6,54},{7,55},{8,56},{9,... | collective-permute-start | bytes 294920 | tf_op jit(solution)/shard_map/ppermute | solution.py:378
  70.7 3.5 %collective-permute-start.8 = (f32[192,128]{1,0:T(8,128)S(1)}, f32[192,128]{1,0:T(8,128)S(1)}, u32[]{:S(2)}, u32[]{:S(2)}) collective-permute-start(f32[192,128]{1,0:T(8,128)S(1)} %slice_add_fusion), channel_id=1, source_target_pairs={{0,64},{1,65},{2,66},{3,67},{4,68},{5,69},{6,70},{7,71},{8,72},{9,... | collective-permute-start | bytes 294920 | tf_op jit(solution)/shard_map/ppermute | solution.py:378
  74.3 3.0 %collective-permute-start.9 = (bf16[192,128]{1,0:T(8,128)(2,1)S(1)}, bf16[192,128]{1,0:T(8,128)(2,1)S(1)}, u32[]{:S(2)}, u32[]{:S(2)}) collective-permute-start(bf16[192,128]{1,0:T(8,128)(2,1)S(1)} %add_convert_fusion), channel_id=1, source_target_pairs={{0,16},{1,17},{2,18},{3,19},{4,20},{5,21},{6,22},{7,23},{8,24},{9,... | collective-permute-start | bytes 147464 | tf_op jit(solution)/shard_map/ppermute | solution.py:378
  77.3 4.1 %collective-permute-start.10 = (bf16[480,128]{1,0:T(8,128)(2,1)S(1)}, bf16[480,128]{1,0:T(8,128)(2,1)S(1)}, u32[]{:S(2)}, u32[]{:S(2)}) collective-permute-start(bf16[480,128]{1,0:T(8,128)(2,1)S(1)} %pad_maximum_fusion.4), channel_id=1, source_target_pairs={{0,2},{1,3},{2,0},{3,1},{4,6},{5,7},{6,4},{7,5},{8,10},{9,11},{10,... | collective-permute-start | bytes 368648 | tf_op jit(solution)/shard_map/ppermute | solution.py:378
  81.5 10.8 %collective-permute-start.11 = (bf16[960,128]{1,0:T(8,128)(2,1)S(1)}, bf16[960,128]{1,0:T(8,128)(2,1)S(1)}, u32[]{:S(2)}, u32[]{:S(2)}) collective-permute-start(bf16[960,128]{1,0:T(8,128)(2,1)S(1)} %pad_maximum_fusion.2.refs_1_), channel_id=1, source_target_pairs={{0,1},{1,0},{2,3},{3,2},{4,5},{5,4},{6,7},{7,6},{8,9},{9,8},{10,11... | collective-permute-start | bytes 737288 | tf_op jit(solution)/shard_map/ppermute | solution.py:378

commit v3 on v2

--- a/solution.py
+++ b/solution.py
@@ -12,14 +12,14 @@
 PADDED = 1536
 BOTH = ("row", "col")
 ROWS = 48
-GROUP = 24
+GROUP = 8
 
 BF = jnp.bfloat16
 F32 = jnp.float32
 
 
-UNITS = "mmm"
-LAG = 2
+UNITS = "xmx"
+LAG = 1
 
 
 def dot(left, right, dims=((1,), (0,))):
@@ -277,7 +277,7 @@
     is_first = core[0] == 0
     channels = w_rows.shape[1]
     depth = w_rows.shape[0]
-    quarter = PADDED // 4
+    half_rows = PADDED // 2
 
     def fetch(low, high):
         first = jnp.where(is_first, mine[low:high], theirs[low:high])
@@ -286,18 +286,17 @@
 
     def weights(low, high):
         pieces = []
-        for part in range(4):
-            begin, end = max(low - part * quarter, 0), min(high - part * quarter, quarter)
+        for part in range(2):
+            begin, end = max(low - part * half_rows, 0), min(high - part * half_rows, half_rows)
             if begin < end:
-                shift = (part % 2) * (quarter + 2 * tokens)
-                pieces.append(fetch(begin + shift, end + shift)[part // 2].astype(F32))
+                pieces.append(fetch(begin, end)[part].astype(F32))
         return pieces[0] if len(pieces) == 1 else jnp.concatenate(pieces, axis=0)
 
     parts = []
     for kind in range(2):
         pieces = []
         for half in range(2):
-            low = half * (quarter + 2 * tokens) + quarter + kind * tokens
+            low = half_rows + half * 2 * tokens + kind * tokens
             pieces.append(fetch(low, low + tokens))
         parts.append(jnp.concatenate([pieces[0][0], pieces[1][0], pieces[0][1], pieces[1][1]], axis=0))
     back = ((1,), (1,))
@@ -390,6 +389,11 @@
 
 def both_sum(value, mask):
     return value + swap(value, mask)
+
+
+def short_sum(value, mask):
+    own = lax.reduce_precision(value, 8, 7)
+    return own + swap(own.astype(BF), mask).astype(F32)
 
 
 def double(value, place, mask):
@@ -443,7 +447,6 @@
         ln_bias[None, :],
         w_in,
     )
-    cols = lax.ppermute(col_sums.astype(BF), BOTH, turn).astype(F32)
     halves = jnp.concatenate(
         [
             sums.reshape(2, PADDED // 2, channels),
@@ -452,29 +455,30 @@
         axis=1,
     )
     held = halve(halves.reshape(PADDED + row_tok, channels), core, 1)
+    held, col_sums = lax.optimization_barrier((held, col_sums))
+    cols = lax.ppermute(col_sums.astype(BF), BOTH, turn).astype(F32)
     weights, rows = held[: PADDED // 2], held[PADDED // 2 :]
-    quarter = PADDED // 4
+    weights = halve(weights, x_half, 16)
+    eighth = PADDED // 8
     tok = row_tok // 4
     mixed = jnp.concatenate(
         [
-            weights.reshape(2, quarter, channels),
+            weights.reshape(2, eighth, channels),
             rows.reshape(2, tok, channels),
             cols.reshape(2, tok, channels),
         ],
         axis=1,
     )
     held = halve(mixed.reshape(-1, channels), y_half, 2)
-    weights, tokens = halve(held[:quarter], x_half, 16), held[quarter:]
-    eighth = quarter // 2
-    held = jnp.concatenate([weights, tokens], axis=0)
-    held = both_sum(held, 6)
-    held = both_sum(held, 8)
+    held = short_sum(held, 6)
+    held = short_sum(held, 8)
     weights, tokens = held[:eighth], held[eighth:]
     weights = both_sum(weights, 48)
     weights = both_sum(weights, 64)
-    weights = double(weights.astype(BF), x_half, 16)
-    done = jnp.concatenate([weights, tokens.astype(BF)], axis=0)
-    done = double(done, y_half, 2)
+    done = jnp.concatenate([weights, tokens], axis=0).astype(BF)
+    done = double(done, y_half, 2).reshape(2, eighth + 2 * tok, channels)
+    weights = double(done[:, :eighth].reshape(2 * eighth, channels), x_half, 16)
+    done = jnp.concatenate([weights, done[:, eighth:].reshape(4 * tok, channels)], axis=0)
     outs = results(tok, core.reshape(1), done, swap(done, 1), w_rows, w_cols, row_tok)
     grad_single, grad_w_rows, grad_w_cols, grad_table, grad_gain, grad_bias, grad_w_in = outs
     return (

time: 93.7 us -> 87.9 us (0.938)
  starting transfers between devices: 33.9 us -> 29.5 us
  Pallas kernels: 32.4 us -> 29.3 us
  waiting for transfers between devices: 23.6 us -> 25.3 us
    ppermute x10, starting transfers between devices: 27.2 us -> 22.5 us  [swap(): return lax.ppermute(value, BOTH, [(at, at ^ mask) for at in range(128)])]
    pallas_call x1, Pallas kernels: 29.6 us -> 26.5 us  [pair_work(): pl.pallas_call(pair_kernel, grid=(steps,), in_specs=[pl.BlockSpec(memory_...]
    ppermute x1, waiting for transfers between devices: 1.18 us -> 3.17 us  [per_device(): cols = lax.ppermute(col_sums.astype(BF), BOTH, turn).astype(F32)]
where the time goes in v3:
time: 87.9 us; the launch traced here: 87.7 us
  starting transfers between devices  29.5 us (34%)
  Pallas kernels  29.3 us (33%)
  waiting for transfers between devices  25.3 us (29%)
  local copies, waits for them, and re-layouts  2.27 us (3%)
  between operations  0.98 us (1%)
    pallas_call x1, Pallas kernels, pair_work(): pl.pallas_call(pair_kernel, grid=(steps,), in_specs=[pl.BlockSpec(memory_...  26.5 us
    ppermute x10, starting transfers between devices, swap(): return lax.ppermute(value, BOTH, [(at, at ^ mask) for at in range(128)])  22.5 us
    ppermute x10, waiting for transfers between devices, swap(): return lax.ppermute(value, BOTH, [(at, at ^ mask) for at in range(128)])  22.1 us
    ppermute x1, starting transfers between devices, per_device(): lax.ppermute(pick(single, core), BOTH, [(to, at) for at, to in turn])  3.64 us
    ppermute x1, starting transfers between devices, per_device(): cols = lax.ppermute(col_sums.astype(BF), BOTH, turn).astype(F32)  3.29 us
    ppermute x1, waiting for transfers between devices, per_device(): cols = lax.ppermute(col_sums.astype(BF), BOTH, turn).astype(F32)  3.17 us
  transfers between devices with their start and end apart: 12, of which 10 were waited for; matrix products, arithmetic and copies ran while one was open for 1% of the time, Pallas kernels for 2%

profile of v3, /device:TPU:1, one launch (start us, length us, event | category | flops | bytes accessed | tf_op | source)
XLA Modules:
  0.0 87.7 jit_solution(10301565276792088400)
XLA Ops:
  0.7 0.9 %constant_dynamic-slice_fusion = bf16[96,384]{1,0:T(8,128)(2,1)S(1)} fusion(bf16[192,384]{1,0:T(8,128)(2,1)} %single_rows.1, s32[]{:T(128)S(6)} %select_n.91), kind=kLoop, calls=%fused_computation.21 | loop fusion | bytes 147460 | tf_op jit(solution)/shard_map/dynamic_slice | solution.py:382
  1.5 0.0 copy-start.5
  1.6 0.0 copy-start
  1.6 0.0 copy-start.1
  1.6 0.0 copy-start.2
  1.6 0.0 copy-start.3
  1.6 0.0 copy-start.4
  1.6 0.0 copy-start.6
  1.6 0.0 copy-start.7
  1.6 3.6 %collective-permute-start = (bf16[96,384]{1,0:T(8,128)(2,1)S(1)}, bf16[96,384]{1,0:T(8,128)(2,1)S(1)}, u32[]{:S(2)}, u32[]{:S(2)}) collective-permute-start(bf16[96,384]{1,0:T(8,128)(2,1)S(1)} %constant_dynamic-slice_fusion), channel_id=1, source_target_pairs={{4,0},{5,1},{20,2},{21,3},{36,4},{37,5},{52,6},{53,7},{68,8},{69,9... | collective-permute-start | bytes 221192 | tf_op jit(solution)/shard_map/ppermute | solution.py:431
  5.3 1.6 %shard_map.171 = s32[192,96]{1,0:T(8,128)} custom-call(s32[192,96]{1,0:T(8,128)} %res.1, s32[192,96]{1,0:T(8,128)} %tok.1), custom_call_target="tpu_custom_call" | custom-call | flops 10000000000 | bytes 1000000 | tf_op jit(solution)/shard_map/pallas_call | solution.py:352
  6.9 1.0 %reshape.61.bins = s32[4,1,4608]{2,1,0:T(1,128)S(1)} reshape(s32[192,96]{1,0:T(8,128)} %shard_map.171) | data formatting | bytes 147456 | tf_op jit(solution)/shard_map/reshape | solution.py:434
  7.9 0.0 copy-done.5
  7.9 0.1 dynamic_slice.25
  8.0 0.0 collective-permute-done.single_cols
  8.0 0.1 broadcast_in_dim.12.chain_right
  8.1 0.0 copy-done
  8.1 0.0 copy-done.1
  8.1 0.0 copy-done.2
  8.1 0.0 copy-done.3
  8.1 0.0 copy-done.4
  8.1 0.0 copy-done.6
  8.2 0.0 copy-done.7
  8.2 26.5 %shard_map.172 = (f32[1536,128]{1,0:T(8,128)S(1)}, f32[192,128]{1,0:T(8,128)S(1)}, f32[96,128]{1,0:T(8,128)S(1)}) custom-call(s32[1536]{0:T(1024)S(1)} %copy-done.5, s32[4,1,4608]{2,1,0:T(1,128)S(1)} %reshape.61.bins, bf16[192,96,256]{2,1,0:T(8,128)(2,1)} %cot_ab.1, bf16[192,96,128]{2,1,0:T(8,128)(2,1)} %cot_z.1, bf16[192,384]{1,0:T(8,128)(2,1)S(1)} %copy-done.2, ...), custom_call_target="tpu_custom_call" | custom-call | flops 8999999488 | bytes 15000000 | tf_op jit(solution)/shard_map/pallas_call | solution.py:242
  34.7 0.1 pad_maximum_fusion
  34.8 1.0 %collective-permute-start.1 = (bf16[864,128]{1,0:T(8,128)(2,1)S(1)}, bf16[864,128]{1,0:T(8,128)(2,1)S(1)}, u32[]{:S(2)}, u32[]{:S(2)}) collective-permute-start(bf16[864,128]{1,0:T(8,128)(2,1)S(1)} %dynamic-slice_convert_fusion), channel_id=1, source_target_pairs={{0,1},{1,0},{2,3},{3,2},{4,5},{5,4},{6,7},{7,6},{8,9},{9,8},{10,11... | collective-permute-start | bytes 663560 | tf_op jit(solution)/shard_map/ppermute | solution.py:377
  35.8 1.1 %collective-permute-done.1 = bf16[864,128]{1,0:T(8,128)(2,1)S(1)} collective-permute-done((bf16[864,128]{1,0:T(8,128)(2,1)S(1)}, bf16[864,128]{1,0:T(8,128)(2,1)S(1)}, u32[]{:S(2)}, u32[]{:S(2)}) %collective-permute-start.1) | collective-permute-done | bytes 221216 | tf_op jit(solution)/shard_map/ppermute | solution.py:377
  37.1 2.0 %collective-permute-start.2 = (bf16[384,128]{1,0:T(8,128)(2,1)S(1)}, bf16[384,128]{1,0:T(8,128)(2,1)S(1)}, u32[]{:S(2)}, u32[]{:S(2)}) collective-permute-start(bf16[384,128]{1,0:T(8,128)(2,1)S(1)} %dynamic-slice_convert_fusion.1), channel_id=1, source_target_pairs={{0,16},{1,17},{2,18},{3,19},{4,20},{5,21},{6,22},{7,23},{8,24},{9,... | collective-permute-start | bytes 294920 | tf_op jit(solution)/shard_map/ppermute | solution.py:377
  39.0 3.3 %collective-permute-start.3 = (bf16[96,128]{1,0:T(8,128)(2,1)S(1)}, bf16[96,128]{1,0:T(8,128)(2,1)S(1)}, u32[]{:S(2)}, u32[]{:S(2)}) collective-permute-start(bf16[96,128]{1,0:T(8,128)(2,1)S(1)} %convert_element_type.39), channel_id=1, source_target_pairs={{0,4},{1,5},{2,20},{3,21},{4,36},{5,37},{6,52},{7,53},{8,68},{9,69... | collective-permute-start | bytes 73736 | tf_op jit(solution)/shard_map/ppermute | solution.py:459
  42.3 3.2 %collective-permute-done.3 = bf16[96,128]{1,0:T(8,128)(2,1)S(1)} collective-permute-done((bf16[96,128]{1,0:T(8,128)(2,1)S(1)}, bf16[96,128]{1,0:T(8,128)(2,1)S(1)}, u32[]{:S(2)}, u32[]{:S(2)}) %collective-permute-start.3) | collective-permute-done | bytes 24608 | tf_op jit(solution)/shard_map/ppermute | solution.py:459
  45.5 0.0 collective-permute-done.2
  45.6 0.1 collective-permute-start.4
  45.7 3.2 %collective-permute-done.4 = bf16[288,128]{1,0:T(8,128)(2,1)S(1)} collective-permute-done((bf16[288,128]{1,0:T(8,128)(2,1)S(1)}, bf16[288,128]{1,0:T(8,128)(2,1)S(1)}, u32[]{:S(2)}, u32[]{:S(2)}) %collective-permute-start.4) | collective-permute-done | bytes 73760 | tf_op jit(solution)/shard_map/ppermute | solution.py:377
  48.9 0.8 collective-permute-start.5
  49.8 3.7 %collective-permute-done.5 = bf16[288,128]{1,0:T(8,128)(2,1)S(1)} collective-permute-done((bf16[288,128]{1,0:T(8,128)(2,1)S(1)}, bf16[288,128]{1,0:T(8,128)(2,1)S(1)}, u32[]{:S(2)}, u32[]{:S(2)}) %collective-permute-start.5) | collective-permute-done | bytes 73760 | tf_op jit(solution)/shard_map/ppermute | solution.py:377
  53.4 4.1 %collective-permute-start.6 = (bf16[288,128]{1,0:T(8,128)(2,1)S(1)}, bf16[288,128]{1,0:T(8,128)(2,1)S(1)}, u32[]{:S(2)}, u32[]{:S(2)}) collective-permute-start(bf16[288,128]{1,0:T(8,128)(2,1)S(1)} %fusion), channel_id=1, source_target_pairs={{0,8},{1,9},{2,10},{3,11},{4,12},{5,13},{6,14},{7,15},{8,0},{9,1},... | collective-permute-start | bytes 221192 | tf_op jit(solution)/shard_map/ppermute | solution.py:377
  57.6 1.7 %collective-permute-done.6 = bf16[288,128]{1,0:T(8,128)(2,1)S(1)} collective-permute-done((bf16[288,128]{1,0:T(8,128)(2,1)S(1)}, bf16[288,128]{1,0:T(8,128)(2,1)S(1)}, u32[]{:S(2)}, u32[]{:S(2)}) %collective-permute-start.6) | collective-permute-done | bytes 73760 | tf_op jit(solution)/shard_map/ppermute | solution.py:377
  59.4 2.4 %collective-permute-start.7 = (f32[192,128]{1,0:T(8,128)S(1)}, f32[192,128]{1,0:T(8,128)S(1)}, u32[]{:S(2)}, u32[]{:S(2)}) collective-permute-start(f32[192,128]{1,0:T(8,128)S(1)} %slice.25), channel_id=1, source_target_pairs={{0,48},{1,49},{2,50},{3,51},{4,52},{5,53},{6,54},{7,55},{8,56},{9,... | collective-permute-start | bytes 294920 | tf_op jit(solution)/shard_map/ppermute | solution.py:377
  61.7 2.4 %collective-permute-done.7 = f32[192,128]{1,0:T(8,128)S(1)} collective-permute-done((f32[192,128]{1,0:T(8,128)S(1)}, f32[192,128]{1,0:T(8,128)S(1)}, u32[]{:S(2)}, u32[]{:S(2)}) %collective-permute-start.7) | collective-permute-done | bytes 98336 | tf_op jit(solution)/shard_map/ppermute | solution.py:377
  64.1 2.9 %collective-permute-start.8 = (f32[192,128]{1,0:T(8,128)S(1)}, f32[192,128]{1,0:T(8,128)S(1)}, u32[]{:S(2)}, u32[]{:S(2)}) collective-permute-start(f32[192,128]{1,0:T(8,128)S(1)} %slice_add_fusion), channel_id=1, source_target_pairs={{0,64},{1,65},{2,66},{3,67},{4,68},{5,69},{6,70},{7,71},{8,72},{9,... | collective-permute-start | bytes 294920 | tf_op jit(solution)/shard_map/ppermute | solution.py:377
  67.0 2.3 %collective-permute-done.8 = f32[192,128]{1,0:T(8,128)S(1)} collective-permute-done((f32[192,128]{1,0:T(8,128)S(1)}, f32[192,128]{1,0:T(8,128)S(1)}, u32[]{:S(2)}, u32[]{:S(2)}) %collective-permute-start.8) | collective-permute-done | bytes 98336 | tf_op jit(solution)/shard_map/ppermute | solution.py:377
  69.4 0.1 collective-permute-start.9
  69.5 3.2 %collective-permute-done.9 = bf16[288,128]{1,0:T(8,128)(2,1)S(1)} collective-permute-done((bf16[288,128]{1,0:T(8,128)(2,1)S(1)}, bf16[288,128]{1,0:T(8,128)(2,1)S(1)}, u32[]{:S(2)}, u32[]{:S(2)}) %collective-permute-start.9) | collective-permute-done | bytes 73760 | tf_op jit(solution)/shard_map/ppermute | solution.py:377
  72.7 0.1 collective-permute-start.10
  72.8 3.4 %collective-permute-done.10 = bf16[384,128]{1,0:T(8,128)(2,1)S(1)} collective-permute-done((bf16[384,128]{1,0:T(8,128)(2,1)S(1)}, bf16[384,128]{1,0:T(8,128)(2,1)S(1)}, u32[]{:S(2)}, u32[]{:S(2)}) %collective-permute-start.10) | collective-permute-done | bytes 98336 | tf_op jit(solution)/shard_map/ppermute | solution.py:377
  76.3 9.0 %collective-permute-start.11 = (bf16[960,128]{1,0:T(8,128)(2,1)S(1)}, bf16[960,128]{1,0:T(8,128)(2,1)S(1)}, u32[]{:S(2)}, u32[]{:S(2)}) collective-permute-start(bf16[960,128]{1,0:T(8,128)(2,1)S(1)} %pad_maximum_fusion.2.refs_1_), channel_id=1, source_target_pairs={{0,1},{1,0},{2,3},{3,2},{4,5},{5,4},{6,7},{7,6},{8,9},{9,8},{10,11... | collective-permute-start | bytes 737288 | tf_op jit(solution)/shard_map/ppermute | solution.py:377
  85.4 1.1 %collective-permute-done.11.refs_2_ = bf16[960,128]{1,0:T(8,128)(2,1)S(1)} collective-permute-done((bf16[960,128]{1,0:T(8,128)(2,1)S(1)}, bf16[960,128]{1,0:T(8,128)(2,1)S(1)}, u32[]{:S(2)}, u32[]{:S(2)}) %collective-permute-start.11) | collective-permute-done | bytes 245792 | tf_op jit(solution)/shard_map/ppermute | solution.py:377
  86.5 1.2 %shard_map.173 = (f32[192,384]{1,0:T(8,128)}, f32[384,128]{1,0:T(8,128)}, f32[384,128]{1,0:T(8,128)}, f32[138,128]{1,0:T(8,128)}, f32[1,128]{1,0:T(1,128)}, /*index=5*/f32[1,128]{1,0:T(1,128)}, f32[128,512]{1,0:T(8,128)}) custom-call(s32[1]{0:T(128)} %bitcast.refs_0_, bf16[960,128]{1,0:T(8,128)(2,1)S(1)} %pad_maximum_fusion.2.refs_1_, ...), custom_call_target="tpu_custom_call" | custom-call | tf_op jit(solution)/shard_map/pallas_call | solution.py:337
  (24 shorter events, 0.4 us)
Async XLA Ops:
  1.5 6.4 %copy-start.5 = (s32[1536]{0:T(1024)S(1)}, s32[1536]{0:T(1024)}, u32[]{:S(2)}) copy-start(s32[1536]{0:T(1024)} %chain_ids.1) | copy-start | bytes 18436
  1.6 6.5 %copy-start = (bf16[384,128]{1,0:T(8,128)(2,1)S(1)}, bf16[384,128]{1,0:T(8,128)(2,1)}, u32[]{:S(2)}) copy-start(bf16[384,128]{1,0:T(8,128)(2,1)} %refs_3_.1) | copy-start | bytes 294916
  1.6 6.5 %copy-start.1 = (bf16[384,128]{1,0:T(8,128)(2,1)S(1)}, bf16[384,128]{1,0:T(8,128)(2,1)}, u32[]{:S(2)}) copy-start(bf16[384,128]{1,0:T(8,128)(2,1)} %refs_4_.1) | copy-start | bytes 294916
  1.6 6.5 %copy-start.2 = (bf16[192,384]{1,0:T(8,128)(2,1)S(1)}, bf16[192,384]{1,0:T(8,128)(2,1)}, u32[]{:S(2)}) copy-start(bf16[192,384]{1,0:T(8,128)(2,1)} %single_rows.1) | copy-start | bytes 442372
  1.6 6.5 %copy-start.3 = (bf16[128,512]{1,0:T(8,128)(2,1)S(1)}, bf16[128,512]{1,0:T(8,128)(2,1)}, u32[]{:S(2)}) copy-start(bf16[128,512]{1,0:T(8,128)(2,1)} %w_in.1) | copy-start | bytes 393220
  1.6 6.5 %copy-start.4 = (bf16[138,128]{1,0:T(8,128)(2,1)S(1)}, bf16[138,128]{1,0:T(8,128)(2,1)}, u32[]{:S(2)}) copy-start(bf16[138,128]{1,0:T(8,128)(2,1)} %rel_table.1) | copy-start | bytes 105988
  1.6 6.5 %copy-start.6 = (f32[128]{0:T(128)S(1)}, f32[128]{0:T(128)}, u32[]{:S(2)}) copy-start(f32[128]{0:T(128)} %param.19) | copy-start | bytes 1540
  1.6 6.5 %copy-start.7 = (f32[128]{0:T(128)S(1)}, f32[128]{0:T(128)}, u32[]{:S(2)}) copy-start(f32[128]{0:T(128)} %param.20) | copy-start | bytes 1540
  1.6 6.4 %collective-permute-start = (bf16[96,384]{1,0:T(8,128)(2,1)S(1)}, bf16[96,384]{1,0:T(8,128)(2,1)S(1)}, u32[]{:S(2)}, u32[]{:S(2)}) collective-permute-start(bf16[96,384]{1,0:T(8,128)(2,1)S(1)} %constant_dynamic-slice_fusion), channel_id=1, source_target_pairs={{4,0},{5,1},{20,2},{21,3},{36,4},{37,5},{52,6},{53,7},{68,8},{69,9... | collective-permute-start | bytes 221192 | tf_op jit(solution)/shard_map/ppermute | solution.py:431
  34.8 2.1 %collective-permute-start.1 = (bf16[864,128]{1,0:T(8,128)(2,1)S(1)}, bf16[864,128]{1,0:T(8,128)(2,1)S(1)}, u32[]{:S(2)}, u32[]{:S(2)}) collective-permute-start(bf16[864,128]{1,0:T(8,128)(2,1)S(1)} %dynamic-slice_convert_fusion), channel_id=1, source_target_pairs={{0,1},{1,0},{2,3},{3,2},{4,5},{5,4},{6,7},{7,6},{8,9},{9,8},{10,11... | collective-permute-start | bytes 663560 | tf_op jit(solution)/shard_map/ppermute | solution.py:377
  37.1 8.5 %collective-permute-start.2 = (bf16[384,128]{1,0:T(8,128)(2,1)S(1)}, bf16[384,128]{1,0:T(8,128)(2,1)S(1)}, u32[]{:S(2)}, u32[]{:S(2)}) collective-permute-start(bf16[384,128]{1,0:T(8,128)(2,1)S(1)} %dynamic-slice_convert_fusion.1), channel_id=1, source_target_pairs={{0,16},{1,17},{2,18},{3,19},{4,20},{5,21},{6,22},{7,23},{8,24},{9,... | collective-permute-start | bytes 294920 | tf_op jit(solution)/shard_map/ppermute | solution.py:377
  39.0 6.5 %collective-permute-start.3 = (bf16[96,128]{1,0:T(8,128)(2,1)S(1)}, bf16[96,128]{1,0:T(8,128)(2,1)S(1)}, u32[]{:S(2)}, u32[]{:S(2)}) collective-permute-start(bf16[96,128]{1,0:T(8,128)(2,1)S(1)} %convert_element_type.39), channel_id=1, source_target_pairs={{0,4},{1,5},{2,20},{3,21},{4,36},{5,37},{6,52},{7,53},{8,68},{9,69... | collective-permute-start | bytes 73736 | tf_op jit(solution)/shard_map/ppermute | solution.py:459
  45.6 3.3 %collective-permute-start.4 = (bf16[288,128]{1,0:T(8,128)(2,1)S(1)}, bf16[288,128]{1,0:T(8,128)(2,1)S(1)}, u32[]{:S(2)}, u32[]{:S(2)}) collective-permute-start(bf16[288,128]{1,0:T(8,128)(2,1)S(1)} %dynamic-slice_convert_fusion.2), channel_id=1, source_target_pairs={{0,2},{1,3},{2,0},{3,1},{4,6},{5,7},{6,4},{7,5},{8,10},{9,11},{10,... | collective-permute-start | bytes 221192 | tf_op jit(solution)/shard_map/ppermute | solution.py:377
  48.9 4.5 %collective-permute-start.5 = (bf16[288,128]{1,0:T(8,128)(2,1)S(1)}, bf16[288,128]{1,0:T(8,128)(2,1)S(1)}, u32[]{:S(2)}, u32[]{:S(2)}) collective-permute-start(bf16[288,128]{1,0:T(8,128)(2,1)S(1)} %fusion.1), channel_id=1, source_target_pairs={{0,6},{1,7},{2,4},{3,5},{4,2},{5,3},{6,0},{7,1},{8,14},{9,15},{10,... | collective-permute-start | bytes 221192 | tf_op jit(solution)/shard_map/ppermute | solution.py:377
  53.4 5.9 %collective-permute-start.6 = (bf16[288,128]{1,0:T(8,128)(2,1)S(1)}, bf16[288,128]{1,0:T(8,128)(2,1)S(1)}, u32[]{:S(2)}, u32[]{:S(2)}) collective-permute-start(bf16[288,128]{1,0:T(8,128)(2,1)S(1)} %fusion), channel_id=1, source_target_pairs={{0,8},{1,9},{2,10},{3,11},{4,12},{5,13},{6,14},{7,15},{8,0},{9,1},... | collective-permute-start | bytes 221192 | tf_op jit(solution)/shard_map/ppermute | solution.py:377
  59.4 4.8 %collective-permute-start.7 = (f32[192,128]{1,0:T(8,128)S(1)}, f32[192,128]{1,0:T(8,128)S(1)}, u32[]{:S(2)}, u32[]{:S(2)}) collective-permute-start(f32[192,128]{1,0:T(8,128)S(1)} %slice.25), channel_id=1, source_target_pairs={{0,48},{1,49},{2,50},{3,51},{4,52},{5,53},{6,54},{7,55},{8,56},{9,... | collective-permute-start | bytes 294920 | tf_op jit(solution)/shard_map/ppermute | solution.py:377
  64.1 5.2 %collective-permute-start.8 = (f32[192,128]{1,0:T(8,128)S(1)}, f32[192,128]{1,0:T(8,128)S(1)}, u32[]{:S(2)}, u32[]{:S(2)}) collective-permute-start(f32[192,128]{1,0:T(8,128)S(1)} %slice_add_fusion), channel_id=1, source_target_pairs={{0,64},{1,65},{2,66},{3,67},{4,68},{5,69},{6,70},{7,71},{8,72},{9,... | collective-permute-start | bytes 294920 | tf_op jit(solution)/shard_map/ppermute | solution.py:377
  69.4 3.3 %collective-permute-start.9 = (bf16[288,128]{1,0:T(8,128)(2,1)S(1)}, bf16[288,128]{1,0:T(8,128)(2,1)S(1)}, u32[]{:S(2)}, u32[]{:S(2)}) collective-permute-start(bf16[288,128]{1,0:T(8,128)(2,1)S(1)} %pad_maximum_fusion.4), channel_id=1, source_target_pairs={{0,2},{1,3},{2,0},{3,1},{4,6},{5,7},{6,4},{7,5},{8,10},{9,11},{10,... | collective-permute-start | bytes 221192 | tf_op jit(solution)/shard_map/ppermute | solution.py:377
  72.7 3.5 %collective-permute-start.10 = (bf16[384,128]{1,0:T(8,128)(2,1)S(1)}, bf16[384,128]{1,0:T(8,128)(2,1)S(1)}, u32[]{:S(2)}, u32[]{:S(2)}) collective-permute-start(bf16[384,128]{1,0:T(8,128)(2,1)S(1)} %bitcast.31), channel_id=1, source_target_pairs={{0,16},{1,17},{2,18},{3,19},{4,20},{5,21},{6,22},{7,23},{8,24},{9,... | collective-permute-start | bytes 294920 | tf_op jit(solution)/shard_map/ppermute | solution.py:377
  76.3 10.2 %collective-permute-start.11 = (bf16[960,128]{1,0:T(8,128)(2,1)S(1)}, bf16[960,128]{1,0:T(8,128)(2,1)S(1)}, u32[]{:S(2)}, u32[]{:S(2)}) collective-permute-start(bf16[960,128]{1,0:T(8,128)(2,1)S(1)} %pad_maximum_fusion.2.refs_1_), channel_id=1, source_target_pairs={{0,1},{1,0},{2,3},{3,2},{4,5},{5,4},{6,7},{7,6},{8,9},{9,8},{10,11... | collective-permute-start | bytes 737288 | tf_op jit(solution)/shard_map/ppermute | solution.py:377

commit v4 on v3

--- a/solution.py
+++ b/solution.py
@@ -387,10 +387,6 @@
     return pick(value, place) + got.astype(F32)
 
 
-def both_sum(value, mask):
-    return value + swap(value, mask)
-
-
 def short_sum(value, mask):
     own = lax.reduce_precision(value, 8, 7)
     return own + swap(own.astype(BF), mask).astype(F32)
@@ -454,7 +450,8 @@
         ],
         axis=1,
     )
-    held = halve(halves.reshape(PADDED + row_tok, channels), core, 1)
+    halves = halves.reshape(PADDED + row_tok, channels)
+    held = pick(halves, core) + swap(pick(halves, 1 - core), 1)
     held, col_sums = lax.optimization_barrier((held, col_sums))
     cols = lax.ppermute(col_sums.astype(BF), BOTH, turn).astype(F32)
     weights, rows = held[: PADDED // 2], held[PADDED // 2 :]
@@ -473,8 +470,8 @@
     held = short_sum(held, 6)
     held = short_sum(held, 8)
     weights, tokens = held[:eighth], held[eighth:]
-    weights = both_sum(weights, 48)
-    weights = both_sum(weights, 64)
+    weights = short_sum(weights, 48)
+    weights = short_sum(weights, 64)
     done = jnp.concatenate([weights, tokens], axis=0).astype(BF)
     done = double(done, y_half, 2).reshape(2, eighth + 2 * tok, channels)
     weights = double(done[:, :eighth].reshape(2 * eighth, channels), x_half, 16)

time: 87.9 us -> 87.2 us (level)
  no operation moved by 1% of the time
where the time goes in v4:
time: 87.2 us; the launch traced here: 87 us
  starting transfers between devices  29.5 us (34%)
  Pallas kernels  29.3 us (34%)
  waiting for transfers between devices  24.6 us (28%)
  local copies, waits for them, and re-layouts  2.27 us (3%)
  between operations  0.98 us (1%)
    pallas_call x1, Pallas kernels, pair_work(): pl.pallas_call(pair_kernel, grid=(steps,), in_specs=[pl.BlockSpec(memory_...  26.5 us
    ppermute x10, starting transfers between devices, swap(): return lax.ppermute(value, BOTH, [(at, at ^ mask) for at in range(128)])  22.5 us
    ppermute x10, waiting for transfers between devices, swap(): return lax.ppermute(value, BOTH, [(at, at ^ mask) for at in range(128)])  21.4 us
    ppermute x1, starting transfers between devices, per_device(): lax.ppermute(pick(single, core), BOTH, [(to, at) for at, to in turn])  3.64 us
    ppermute x1, starting transfers between devices, per_device(): cols = lax.ppermute(col_sums.astype(BF), BOTH, turn).astype(F32)  3.29 us
    ppermute x1, waiting for transfers between devices, per_device(): cols = lax.ppermute(col_sums.astype(BF), BOTH, turn).astype(F32)  3.16 us
  transfers between devices with their start and end apart: 12, of which 10 were waited for; matrix products, arithmetic and copies ran while one was open for 1% of the time, Pallas kernels for 2%

profile of v4, /device:TPU:1, one launch (start us, length us, event | category | flops | bytes accessed | tf_op | source)
XLA Modules:
  0.0 87.0 jit_solution(16901766920959813208)
XLA Ops:
  0.7 0.9 %constant_dynamic-slice_fusion.1 = bf16[96,384]{1,0:T(8,128)(2,1)S(1)} fusion(bf16[192,384]{1,0:T(8,128)(2,1)} %single_rows.1, s32[]{:T(128)S(6)} %select_n.91), kind=kLoop, calls=%fused_computation.25 | loop fusion | bytes 147460 | tf_op jit(solution)/shard_map/dynamic_slice | solution.py:382
  1.5 0.0 copy-start.5
  1.6 0.0 copy-start
  1.6 0.0 copy-start.1
  1.6 0.0 copy-start.2
  1.6 0.0 copy-start.3
  1.6 0.0 copy-start.4
  1.6 0.0 copy-start.6
  1.6 0.0 copy-start.7
  1.6 3.6 %collective-permute-start = (bf16[96,384]{1,0:T(8,128)(2,1)S(1)}, bf16[96,384]{1,0:T(8,128)(2,1)S(1)}, u32[]{:S(2)}, u32[]{:S(2)}) collective-permute-start(bf16[96,384]{1,0:T(8,128)(2,1)S(1)} %constant_dynamic-slice_fusion.1), channel_id=1, source_target_pairs={{4,0},{5,1},{20,2},{21,3},{36,4},{37,5},{52,6},{53,7},{68,8},{69,9... | collective-permute-start | bytes 221192 | tf_op jit(solution)/shard_map/ppermute | solution.py:427
  5.3 1.6 %shard_map.171 = s32[192,96]{1,0:T(8,128)} custom-call(s32[192,96]{1,0:T(8,128)} %res.1, s32[192,96]{1,0:T(8,128)} %tok.1), custom_call_target="tpu_custom_call" | custom-call | flops 10000000000 | bytes 1000000 | tf_op jit(solution)/shard_map/pallas_call | solution.py:352
  6.9 1.0 %reshape.61.bins = s32[4,1,4608]{2,1,0:T(1,128)S(1)} reshape(s32[192,96]{1,0:T(8,128)} %shard_map.171) | data formatting | bytes 147456 | tf_op jit(solution)/shard_map/reshape | solution.py:430
  7.9 0.0 copy-done.5
  7.9 0.1 dynamic_slice.25
  8.0 0.0 collective-permute-done.single_cols
  8.0 0.1 broadcast_in_dim.12.chain_right
  8.1 0.0 copy-done
  8.1 0.0 copy-done.1
  8.1 0.0 copy-done.2
  8.1 0.0 copy-done.3
  8.1 0.0 copy-done.4
  8.1 0.0 copy-done.6
  8.2 0.0 copy-done.7
  8.2 26.5 %shard_map.172 = (f32[1536,128]{1,0:T(8,128)S(1)}, f32[192,128]{1,0:T(8,128)S(1)}, f32[96,128]{1,0:T(8,128)S(1)}) custom-call(s32[1536]{0:T(1024)S(1)} %copy-done.5, s32[4,1,4608]{2,1,0:T(1,128)S(1)} %reshape.61.bins, bf16[192,96,256]{2,1,0:T(8,128)(2,1)} %cot_ab.1, bf16[192,96,128]{2,1,0:T(8,128)(2,1)} %cot_z.1, bf16[192,384]{1,0:T(8,128)(2,1)S(1)} %copy-done.2, ...), custom_call_target="tpu_custom_call" | custom-call | flops 8999999488 | bytes 15000000 | tf_op jit(solution)/shard_map/pallas_call | solution.py:242
  34.7 0.1 pad_maximum_fusion
  34.8 1.0 %collective-permute-start.1 = (f32[864,128]{1,0:T(8,128)S(1)}, f32[864,128]{1,0:T(8,128)S(1)}, u32[]{:S(2)}, u32[]{:S(2)}) collective-permute-start(f32[864,128]{1,0:T(8,128)S(1)} %constant_dynamic-slice_fusion), channel_id=1, source_target_pairs={{0,1},{1,0},{2,3},{3,2},{4,5},{5,4},{6,7},{7,6},{8,9},{9,8},{10,11... | collective-permute-start | bytes 1327112 | tf_op jit(solution)/shard_map/ppermute | solution.py:377
  35.9 1.4 %collective-permute-done.1 = f32[864,128]{1,0:T(8,128)S(1)} collective-permute-done((f32[864,128]{1,0:T(8,128)S(1)}, f32[864,128]{1,0:T(8,128)S(1)}, u32[]{:S(2)}, u32[]{:S(2)}) %collective-permute-start.1) | collective-permute-done | bytes 442400 | tf_op jit(solution)/shard_map/ppermute | solution.py:377
  37.4 2.0 %collective-permute-start.2 = (bf16[384,128]{1,0:T(8,128)(2,1)S(1)}, bf16[384,128]{1,0:T(8,128)(2,1)S(1)}, u32[]{:S(2)}, u32[]{:S(2)}) collective-permute-start(bf16[384,128]{1,0:T(8,128)(2,1)S(1)} %dynamic-slice_convert_fusion), channel_id=1, source_target_pairs={{0,16},{1,17},{2,18},{3,19},{4,20},{5,21},{6,22},{7,23},{8,24},{9,... | collective-permute-start | bytes 294920 | tf_op jit(solution)/shard_map/ppermute | solution.py:377
  39.4 3.3 %collective-permute-start.3 = (bf16[96,128]{1,0:T(8,128)(2,1)S(1)}, bf16[96,128]{1,0:T(8,128)(2,1)S(1)}, u32[]{:S(2)}, u32[]{:S(2)}) collective-permute-start(bf16[96,128]{1,0:T(8,128)(2,1)S(1)} %convert_element_type.43), channel_id=1, source_target_pairs={{0,4},{1,5},{2,20},{3,21},{4,36},{5,37},{6,52},{7,53},{8,68},{9,69... | collective-permute-start | bytes 73736 | tf_op jit(solution)/shard_map/ppermute | solution.py:456
  42.7 3.2 %collective-permute-done.3 = bf16[96,128]{1,0:T(8,128)(2,1)S(1)} collective-permute-done((bf16[96,128]{1,0:T(8,128)(2,1)S(1)}, bf16[96,128]{1,0:T(8,128)(2,1)S(1)}, u32[]{:S(2)}, u32[]{:S(2)}) %collective-permute-start.3) | collective-permute-done | bytes 24608 | tf_op jit(solution)/shard_map/ppermute | solution.py:456
  45.8 0.0 collective-permute-done.2
  45.9 0.1 collective-permute-start.4
  46.0 3.2 %collective-permute-done.4 = bf16[288,128]{1,0:T(8,128)(2,1)S(1)} collective-permute-done((bf16[288,128]{1,0:T(8,128)(2,1)S(1)}, bf16[288,128]{1,0:T(8,128)(2,1)S(1)}, u32[]{:S(2)}, u32[]{:S(2)}) %collective-permute-start.4) | collective-permute-done | bytes 73760 | tf_op jit(solution)/shard_map/ppermute | solution.py:377
  49.2 0.8 collective-permute-start.5
  50.1 3.6 %collective-permute-done.5 = bf16[288,128]{1,0:T(8,128)(2,1)S(1)} collective-permute-done((bf16[288,128]{1,0:T(8,128)(2,1)S(1)}, bf16[288,128]{1,0:T(8,128)(2,1)S(1)}, u32[]{:S(2)}, u32[]{:S(2)}) %collective-permute-start.5) | collective-permute-done | bytes 73760 | tf_op jit(solution)/shard_map/ppermute | solution.py:377
  53.8 4.1 %collective-permute-start.6 = (bf16[288,128]{1,0:T(8,128)(2,1)S(1)}, bf16[288,128]{1,0:T(8,128)(2,1)S(1)}, u32[]{:S(2)}, u32[]{:S(2)}) collective-permute-start(bf16[288,128]{1,0:T(8,128)(2,1)S(1)} %fusion), channel_id=1, source_target_pairs={{0,8},{1,9},{2,10},{3,11},{4,12},{5,13},{6,14},{7,15},{8,0},{9,1},... | collective-permute-start | bytes 221192 | tf_op jit(solution)/shard_map/ppermute | solution.py:377
  57.9 1.7 %collective-permute-done.6 = bf16[288,128]{1,0:T(8,128)(2,1)S(1)} collective-permute-done((bf16[288,128]{1,0:T(8,128)(2,1)S(1)}, bf16[288,128]{1,0:T(8,128)(2,1)S(1)}, u32[]{:S(2)}, u32[]{:S(2)}) %collective-permute-start.6) | collective-permute-done | bytes 73760 | tf_op jit(solution)/shard_map/ppermute | solution.py:377
  59.7 2.4 %collective-permute-start.7 = (bf16[192,128]{1,0:T(8,128)(2,1)S(1)}, bf16[192,128]{1,0:T(8,128)(2,1)S(1)}, u32[]{:S(2)}, u32[]{:S(2)}) collective-permute-start(bf16[192,128]{1,0:T(8,128)(2,1)S(1)} %fusion.1), channel_id=1, source_target_pairs={{0,48},{1,49},{2,50},{3,51},{4,52},{5,53},{6,54},{7,55},{8,56},{9,... | collective-permute-start | bytes 147464 | tf_op jit(solution)/shard_map/ppermute | solution.py:377
  62.1 1.9 %collective-permute-done.7 = bf16[192,128]{1,0:T(8,128)(2,1)S(1)} collective-permute-done((bf16[192,128]{1,0:T(8,128)(2,1)S(1)}, bf16[192,128]{1,0:T(8,128)(2,1)S(1)}, u32[]{:S(2)}, u32[]{:S(2)}) %collective-permute-start.7) | collective-permute-done | bytes 49184 | tf_op jit(solution)/shard_map/ppermute | solution.py:377
  64.0 3.0 %collective-permute-start.8 = (bf16[192,128]{1,0:T(8,128)(2,1)S(1)}, bf16[192,128]{1,0:T(8,128)(2,1)S(1)}, u32[]{:S(2)}, u32[]{:S(2)}) collective-permute-start(bf16[192,128]{1,0:T(8,128)(2,1)S(1)} %fusion.2), channel_id=1, source_target_pairs={{0,64},{1,65},{2,66},{3,67},{4,68},{5,69},{6,70},{7,71},{8,72},{9,... | collective-permute-start | bytes 147464 | tf_op jit(solution)/shard_map/ppermute | solution.py:377
  67.0 1.8 %collective-permute-done.8 = bf16[192,128]{1,0:T(8,128)(2,1)S(1)} collective-permute-done((bf16[192,128]{1,0:T(8,128)(2,1)S(1)}, bf16[192,128]{1,0:T(8,128)(2,1)S(1)}, u32[]{:S(2)}, u32[]{:S(2)}) %collective-permute-start.8) | collective-permute-done | bytes 49184 | tf_op jit(solution)/shard_map/ppermute | solution.py:377
  68.8 0.1 collective-permute-start.9
  68.9 3.2 %collective-permute-done.9 = bf16[288,128]{1,0:T(8,128)(2,1)S(1)} collective-permute-done((bf16[288,128]{1,0:T(8,128)(2,1)S(1)}, bf16[288,128]{1,0:T(8,128)(2,1)S(1)}, u32[]{:S(2)}, u32[]{:S(2)}) %collective-permute-start.9) | collective-permute-done | bytes 73760 | tf_op jit(solution)/shard_map/ppermute | solution.py:377
  72.2 0.1 collective-permute-start.10
  72.3 3.4 %collective-permute-done.10 = bf16[384,128]{1,0:T(8,128)(2,1)S(1)} collective-permute-done((bf16[384,128]{1,0:T(8,128)(2,1)S(1)}, bf16[384,128]{1,0:T(8,128)(2,1)S(1)}, u32[]{:S(2)}, u32[]{:S(2)}) %collective-permute-start.10) | collective-permute-done | bytes 98336 | tf_op jit(solution)/shard_map/ppermute | solution.py:377
  75.8 8.9 %collective-permute-start.11 = (bf16[960,128]{1,0:T(8,128)(2,1)S(1)}, bf16[960,128]{1,0:T(8,128)(2,1)S(1)}, u32[]{:S(2)}, u32[]{:S(2)}) collective-permute-start(bf16[960,128]{1,0:T(8,128)(2,1)S(1)} %pad_maximum_fusion.2.refs_1_), channel_id=1, source_target_pairs={{0,1},{1,0},{2,3},{3,2},{4,5},{5,4},{6,7},{7,6},{8,9},{9,8},{10,11... | collective-permute-start | bytes 737288 | tf_op jit(solution)/shard_map/ppermute | solution.py:377
  84.7 1.1 %collective-permute-done.11.refs_2_ = bf16[960,128]{1,0:T(8,128)(2,1)S(1)} collective-permute-done((bf16[960,128]{1,0:T(8,128)(2,1)S(1)}, bf16[960,128]{1,0:T(8,128)(2,1)S(1)}, u32[]{:S(2)}, u32[]{:S(2)}) %collective-permute-start.11) | collective-permute-done | bytes 245792 | tf_op jit(solution)/shard_map/ppermute | solution.py:377
  85.8 1.2 %shard_map.173 = (f32[192,384]{1,0:T(8,128)}, f32[384,128]{1,0:T(8,128)}, f32[384,128]{1,0:T(8,128)}, f32[138,128]{1,0:T(8,128)}, f32[1,128]{1,0:T(1,128)}, /*index=5*/f32[1,128]{1,0:T(1,128)}, f32[128,512]{1,0:T(8,128)}) custom-call(s32[1]{0:T(128)} %bitcast.refs_0_, bf16[960,128]{1,0:T(8,128)(2,1)S(1)} %pad_maximum_fusion.2.refs_1_, ...), custom_call_target="tpu_custom_call" | custom-call | tf_op jit(solution)/shard_map/pallas_call | solution.py:337
  (24 shorter events, 0.5 us)
Async XLA Ops:
  1.5 6.4 %copy-start.5 = (s32[1536]{0:T(1024)S(1)}, s32[1536]{0:T(1024)}, u32[]{:S(2)}) copy-start(s32[1536]{0:T(1024)} %chain_ids.1) | copy-start | bytes 18436
  1.6 6.5 %copy-start = (bf16[384,128]{1,0:T(8,128)(2,1)S(1)}, bf16[384,128]{1,0:T(8,128)(2,1)}, u32[]{:S(2)}) copy-start(bf16[384,128]{1,0:T(8,128)(2,1)} %refs_3_.1) | copy-start | bytes 294916
  1.6 6.5 %copy-start.1 = (bf16[384,128]{1,0:T(8,128)(2,1)S(1)}, bf16[384,128]{1,0:T(8,128)(2,1)}, u32[]{:S(2)}) copy-start(bf16[384,128]{1,0:T(8,128)(2,1)} %refs_4_.1) | copy-start | bytes 294916
  1.6 6.5 %copy-start.2 = (bf16[192,384]{1,0:T(8,128)(2,1)S(1)}, bf16[192,384]{1,0:T(8,128)(2,1)}, u32[]{:S(2)}) copy-start(bf16[192,384]{1,0:T(8,128)(2,1)} %single_rows.1) | copy-start | bytes 442372
  1.6 6.5 %copy-start.3 = (bf16[128,512]{1,0:T(8,128)(2,1)S(1)}, bf16[128,512]{1,0:T(8,128)(2,1)}, u32[]{:S(2)}) copy-start(bf16[128,512]{1,0:T(8,128)(2,1)} %w_in.1) | copy-start | bytes 393220
  1.6 6.5 %copy-start.4 = (bf16[138,128]{1,0:T(8,128)(2,1)S(1)}, bf16[138,128]{1,0:T(8,128)(2,1)}, u32[]{:S(2)}) copy-start(bf16[138,128]{1,0:T(8,128)(2,1)} %rel_table.1) | copy-start | bytes 105988
  1.6 6.5 %copy-start.6 = (f32[128]{0:T(128)S(1)}, f32[128]{0:T(128)}, u32[]{:S(2)}) copy-start(f32[128]{0:T(128)} %param.19) | copy-start | bytes 1540
  1.6 6.5 %copy-start.7 = (f32[128]{0:T(128)S(1)}, f32[128]{0:T(128)}, u32[]{:S(2)}) copy-start(f32[128]{0:T(128)} %param.20) | copy-start | bytes 1540
  1.6 6.4 %collective-permute-start = (bf16[96,384]{1,0:T(8,128)(2,1)S(1)}, bf16[96,384]{1,0:T(8,128)(2,1)S(1)}, u32[]{:S(2)}, u32[]{:S(2)}) collective-permute-start(bf16[96,384]{1,0:T(8,128)(2,1)S(1)} %constant_dynamic-slice_fusion.1), channel_id=1, source_target_pairs={{4,0},{5,1},{20,2},{21,3},{36,4},{37,5},{52,6},{53,7},{68,8},{69,9... | collective-permute-start | bytes 221192 | tf_op jit(solution)/shard_map/ppermute | solution.py:427
  34.8 2.5 %collective-permute-start.1 = (f32[864,128]{1,0:T(8,128)S(1)}, f32[864,128]{1,0:T(8,128)S(1)}, u32[]{:S(2)}, u32[]{:S(2)}) collective-permute-start(f32[864,128]{1,0:T(8,128)S(1)} %constant_dynamic-slice_fusion), channel_id=1, source_target_pairs={{0,1},{1,0},{2,3},{3,2},{4,5},{5,4},{6,7},{7,6},{8,9},{9,8},{10,11... | collective-permute-start | bytes 1327112 | tf_op jit(solution)/shard_map/ppermute | solution.py:377
  37.4 8.4 %collective-permute-start.2 = (bf16[384,128]{1,0:T(8,128)(2,1)S(1)}, bf16[384,128]{1,0:T(8,128)(2,1)S(1)}, u32[]{:S(2)}, u32[]{:S(2)}) collective-permute-start(bf16[384,128]{1,0:T(8,128)(2,1)S(1)} %dynamic-slice_convert_fusion), channel_id=1, source_target_pairs={{0,16},{1,17},{2,18},{3,19},{4,20},{5,21},{6,22},{7,23},{8,24},{9,... | collective-permute-start | bytes 294920 | tf_op jit(solution)/shard_map/ppermute | solution.py:377
  39.4 6.5 %collective-permute-start.3 = (bf16[96,128]{1,0:T(8,128)(2,1)S(1)}, bf16[96,128]{1,0:T(8,128)(2,1)S(1)}, u32[]{:S(2)}, u32[]{:S(2)}) collective-permute-start(bf16[96,128]{1,0:T(8,128)(2,1)S(1)} %convert_element_type.43), channel_id=1, source_target_pairs={{0,4},{1,5},{2,20},{3,21},{4,36},{5,37},{6,52},{7,53},{8,68},{9,69... | collective-permute-start | bytes 73736 | tf_op jit(solution)/shard_map/ppermute | solution.py:456
  45.9 3.3 %collective-permute-start.4 = (bf16[288,128]{1,0:T(8,128)(2,1)S(1)}, bf16[288,128]{1,0:T(8,128)(2,1)S(1)}, u32[]{:S(2)}, u32[]{:S(2)}) collective-permute-start(bf16[288,128]{1,0:T(8,128)(2,1)S(1)} %dynamic-slice_convert_fusion.1), channel_id=1, source_target_pairs={{0,2},{1,3},{2,0},{3,1},{4,6},{5,7},{6,4},{7,5},{8,10},{9,11},{10,... | collective-permute-start | bytes 221192 | tf_op jit(solution)/shard_map/ppermute | solution.py:377
  49.2 4.5 %collective-permute-start.5 = (bf16[288,128]{1,0:T(8,128)(2,1)S(1)}, bf16[288,128]{1,0:T(8,128)(2,1)S(1)}, u32[]{:S(2)}, u32[]{:S(2)}) collective-permute-start(bf16[288,128]{1,0:T(8,128)(2,1)S(1)} %fusion.3), channel_id=1, source_target_pairs={{0,6},{1,7},{2,4},{3,5},{4,2},{5,3},{6,0},{7,1},{8,14},{9,15},{10,... | collective-permute-start | bytes 221192 | tf_op jit(solution)/shard_map/ppermute | solution.py:377
  53.8 5.9 %collective-permute-start.6 = (bf16[288,128]{1,0:T(8,128)(2,1)S(1)}, bf16[288,128]{1,0:T(8,128)(2,1)S(1)}, u32[]{:S(2)}, u32[]{:S(2)}) collective-permute-start(bf16[288,128]{1,0:T(8,128)(2,1)S(1)} %fusion), channel_id=1, source_target_pairs={{0,8},{1,9},{2,10},{3,11},{4,12},{5,13},{6,14},{7,15},{8,0},{9,1},... | collective-permute-start | bytes 221192 | tf_op jit(solution)/shard_map/ppermute | solution.py:377
  59.7 4.2 %collective-permute-start.7 = (bf16[192,128]{1,0:T(8,128)(2,1)S(1)}, bf16[192,128]{1,0:T(8,128)(2,1)S(1)}, u32[]{:S(2)}, u32[]{:S(2)}) collective-permute-start(bf16[192,128]{1,0:T(8,128)(2,1)S(1)} %fusion.1), channel_id=1, source_target_pairs={{0,48},{1,49},{2,50},{3,51},{4,52},{5,53},{6,54},{7,55},{8,56},{9,... | collective-permute-start | bytes 147464 | tf_op jit(solution)/shard_map/ppermute | solution.py:377
  64.0 4.8 %collective-permute-start.8 = (bf16[192,128]{1,0:T(8,128)(2,1)S(1)}, bf16[192,128]{1,0:T(8,128)(2,1)S(1)}, u32[]{:S(2)}, u32[]{:S(2)}) collective-permute-start(bf16[192,128]{1,0:T(8,128)(2,1)S(1)} %fusion.2), channel_id=1, source_target_pairs={{0,64},{1,65},{2,66},{3,67},{4,68},{5,69},{6,70},{7,71},{8,72},{9,... | collective-permute-start | bytes 147464 | tf_op jit(solution)/shard_map/ppermute | solution.py:377
  68.8 3.3 %collective-permute-start.9 = (bf16[288,128]{1,0:T(8,128)(2,1)S(1)}, bf16[288,128]{1,0:T(8,128)(2,1)S(1)}, u32[]{:S(2)}, u32[]{:S(2)}) collective-permute-start(bf16[288,128]{1,0:T(8,128)(2,1)S(1)} %pad_maximum_fusion.4), channel_id=1, source_target_pairs={{0,2},{1,3},{2,0},{3,1},{4,6},{5,7},{6,4},{7,5},{8,10},{9,11},{10,... | collective-permute-start | bytes 221192 | tf_op jit(solution)/shard_map/ppermute | solution.py:377
  72.2 3.5 %collective-permute-start.10 = (bf16[384,128]{1,0:T(8,128)(2,1)S(1)}, bf16[384,128]{1,0:T(8,128)(2,1)S(1)}, u32[]{:S(2)}, u32[]{:S(2)}) collective-permute-start(bf16[384,128]{1,0:T(8,128)(2,1)S(1)} %bitcast.31), channel_id=1, source_target_pairs={{0,16},{1,17},{2,18},{3,19},{4,20},{5,21},{6,22},{7,23},{8,24},{9,... | collective-permute-start | bytes 294920 | tf_op jit(solution)/shard_map/ppermute | solution.py:377
  75.8 10.0 %collective-permute-start.11 = (bf16[960,128]{1,0:T(8,128)(2,1)S(1)}, bf16[960,128]{1,0:T(8,128)(2,1)S(1)}, u32[]{:S(2)}, u32[]{:S(2)}) collective-permute-start(bf16[960,128]{1,0:T(8,128)(2,1)S(1)} %pad_maximum_fusion.2.refs_1_), channel_id=1, source_target_pairs={{0,1},{1,0},{2,3},{3,2},{4,5},{5,4},{6,7},{7,6},{8,9},{9,8},{10,11... | collective-permute-start | bytes 737288 | tf_op jit(solution)/shard_map/ppermute | solution.py:377
